TPU v7x, 32 devices: a whole 2x2x4 slice. The times are simulated.
32 devices in a mesh: reader: 4 (over y, x), blk: 8 (over z, core).
Axes of the slice: x: 2, y: 2, z: 4, core: 2. Of those that a mesh axis runs over, the one named last changes fastest.
Arguments:
- features: bfloat16 [4096, 512], P(('reader', 'blk')), may hold values from -40 to 40
- cotangent: bfloat16 [4096, 512], P(('reader', 'blk')), may hold values from -6 to 6
- w_query: bfloat16 [512, 512], replicated, may hold values from -0.25 to 0.25
- w_key: bfloat16 [512, 512], replicated, may hold values from -0.25 to 0.25
- w_value: bfloat16 [512, 512], replicated, may hold values from -0.25 to 0.25
- tile_coords: int32 [4, 8, 8, 3], P('reader', 'blk'), may hold values from 0 to 239, as said below
- tile_count: int32 [4, 8], P('reader', 'blk'), may hold values from 1 to 8, as said below
- mask_table: int32 [240, 128, 4], replicated, may hold values from -2147483648 to 2147483647, as said below
Outputs:
- attn_out: bfloat16 [4096, 512], P(('reader', 'blk'))
- grad_features: bfloat16 [4096, 512], P(('reader', 'blk'))
Inputs may be any that keep to these rules, and one draw needn't show every extreme that they name: `tile_coords`: for every r and b the 8 slots name distinct (qb, kb) pairs with qb < 8, kb < 4, p < 240; the first 1 slots are the tiles in which the nodes of segment r * 8 + b meet themselves. `tile_count`: some pair (r, b) uses all 8 slots, and some pair uses the fewest. `mask_table`: each word packs 32 edge bits as a signed int32; each bit is set with probability 1/32.
All inputs are finite; a program needn't handle non-finite values.
Results may differ from a plain program's by a relative error of at most 0.01265.
The roundings to bfloat16 on the way count: a program that leaves them out, or rounds other values in their place, can miss the bound.
Values may be sent and summed in bfloat16 or wider, within the bound.
No kernel may reach another device: no remote copies, remote signals or barrier semaphores. Data moves between devices by JAX's collectives and lax.ppermute only.
A program may use at most 128 MiB of HBM per device.

v0:
```python
import functools

import jax
import jax.numpy as jnp
from jax import lax
from jax.experimental import pallas as pl
from jax.experimental.pallas import tpu as pltpu
from jax.sharding import PartitionSpec as P

HEADS = 8
NEG_FILL = -1e30
NT = (((1,), (1,)), ((), ()))
NN = (((1,), (0,)), ((), ()))
TILES = 2
LIST_ROWS = 16
VMEM_SOME = 40 * 1024 * 1024
VMEM_MOST = 58 * 1024 * 1024


def dot(a, b, dims=NN):
    return lax.dot_general(a, b, dims, preferred_element_type=jnp.float32)


def pair_stack(rows):
    lane = lax.broadcasted_iota(jnp.int32, rows.shape, 1)
    half = rows.shape[1] // 2
    zero = jnp.zeros_like(rows)
    return jnp.concatenate([jnp.where(lane < half, rows, zero), jnp.where(lane >= half, rows, zero)], 0)


def tile_bias(words, pattern, diag):
    count, size = words.shape
    keys = lax.broadcasted_iota(jnp.int32, (size, size), 0)
    queries = lax.broadcasted_iota(jnp.int32, (size, size), 1)
    spread = jnp.concatenate(
        [jnp.broadcast_to(words[g : g + 1], (size // count, size)) for g in range(count)], 0
    )
    bits = jnp.right_shift(spread, keys & 31) & 1
    same = keys - queries == jnp.where(diag, 0, 2 * size)
    return jnp.where((bits == 1) | same, jnp.where(pattern < 0, NEG_FILL, 0.0), NEG_FILL)


class Layout:
    def __init__(self, readers, blks, cap):
        self.readers, self.blks, self.cap = readers, blks, cap
        self.reader, self.blk = lax.axis_index("reader"), lax.axis_index("blk")
        self.me = self.reader * blks + self.blk

    def apart(self, device):
        far = jnp.bitwise_xor(device, self.me)
        reader, blk = far // self.blks, lax.rem(far, self.blks)
        return reader, blk // 2, blk & 1

    def row_place(self, order, device):
        reader, line, core = self.apart(device)
        for at, bit in enumerate(order[:-1]):
            line = line + (jnp.right_shift(reader, bit) & 1) * ((self.blks // 2) << at)
        return (jnp.right_shift(reader, order[-1]) & 1) + 2 * core, line

    def orders(self):
        return orders(self.readers)

    def half_place(self, bit, device):
        reader, line, core = self.apart(device)
        first = jnp.right_shift(reader, bit) & 1
        top = (self.blks // 2 - 1).bit_length() - 1
        line = sum((jnp.right_shift(line, top - at) & 1) << at for at in range(top + 1))
        low = reader & ((1 << bit) - 1)
        rest = low + (jnp.right_shift(reader, bit + 1) << bit)
        return rest + self.readers // 2 * core, 2 * line + first


def orders(readers):
    rising = tuple(range((readers - 1).bit_length()))
    return rising, rising[::-1]


def start_copy(place, refs, make):
    group, where = place
    for g, ref in enumerate(refs):

        @pl.when(group == g)
        def _():
            make(ref.at[where]).start()


def pack_kernel(own_hbm, coords_hbm, count_hbm, out_ref, coords_ref, count_ref, sems):
    block = own_hbm.shape[0]
    cap = coords_ref.shape[3]
    copies = [
        pltpu.make_async_copy(coords_hbm, coords_ref, sems.at[0]),
        pltpu.make_async_copy(count_hbm, count_ref, sems.at[1]),
        pltpu.make_async_copy(own_hbm, out_ref.at[0, pl.ds(0, block)], sems.at[2]),
    ]
    for copy in copies:
        copy.start()
    copies[0].wait()
    copies[1].wait()
    lane = lax.broadcasted_iota(jnp.int32, (LIST_ROWS, out_ref.shape[2]), 1)
    row = jnp.zeros(lane.shape, jnp.int32)
    for column in range(3):
        for slot in range(cap):
            row = jnp.where(lane == column * cap + slot, coords_ref[0, column, 0, slot], row)
    row = jnp.where(lane == 3 * cap, count_ref[0, 0], row)
    out_ref[0, block:] = row.astype(jnp.float32).astype(jnp.bfloat16)
    copies[2].wait()


def scan_list(lists_ref, cap, row, column, wanted, found, out_ref, block_of):
    def one_slot(slot, found):
        out_ref[2 * found + 1] = block_of(lists_ref[row, (1 - column) * cap + slot])
        out_ref[2 * found + 2] = lists_ref[row, 2 * cap + slot]
        return found + jnp.where(lists_ref[row, column * cap + slot] == wanted, 1, 0)

    return lax.fori_loop(0, lists_ref[row, 3 * cap], one_slot, found)


def close_work(found, out_ref):
    out_ref[2 * found + 1] = out_ref[2 * found - 1]
    out_ref[2 * found + 2] = -1
    out_ref[0] = (found + 1) // 2


def query_work_kernel(sizes, lists_hbm, work_ref, lists_ref, sem):
    readers, blks, cap = sizes
    layout = Layout(*sizes)
    copy = pltpu.make_async_copy(lists_hbm, lists_ref, sem)
    copy.start()
    copy.wait()

    def one(k, found):
        blk = jnp.bitwise_xor(k, layout.blk)
        row = k // 2 + (k & 1) * (blks // 2)
        put = lambda other: other * blks + blk
        return scan_list(lists_ref, cap, row, 0, layout.blk, found, work_ref, put)

    close_work(lax.fori_loop(0, blks, one, 0), work_ref)


def key_work_kernel(sizes, lists_hbm, work_ref, lists_ref, sem):
    readers, blks, cap = sizes
    layout = Layout(*sizes)
    copy = pltpu.make_async_copy(lists_hbm, lists_ref, sem)
    copy.start()
    copy.wait()

    def one(k, found):
        reader = jnp.bitwise_xor(k, layout.reader)
        put = lambda other: reader * blks + other
        return scan_list(lists_ref, cap, k, 1, layout.reader, found, work_ref, put)

    close_work(lax.fori_loop(0, readers, one, 0), work_ref)


def load(pairs, sems):
    copies = [pltpu.make_async_copy(src, into, sems.at[k]) for k, (src, into) in enumerate(pairs)]
    for copy in copies:
        copy.start()
    return copies


def prepare_kernel(
    own_hbm, cot_hbm, wq_hbm, wk_hbm, wv_hbm,
    query_stack_ref, cot_stack_ref, key_ref, value_ref, wqt_ref, wkt_ref, wvt_ref,
    own_ref, cot_ref, wq_ref, wk_ref, wv_ref, sems,
):
    loads = load((
        (own_hbm, own_ref), (wq_hbm, wq_ref), (wk_hbm, wk_ref), (wv_hbm, wv_ref), (cot_hbm, cot_ref),
    ), sems)
    for copy in loads:
        copy.wait()
    head = own_ref.shape[1] // HEADS
    queries = dot(own_ref[...], wq_ref[...]).astype(jnp.bfloat16) * jnp.bfloat16(head**-0.5)
    for p in range(HEADS // 2):
        pair = slice(2 * head * p, 2 * head * (p + 1))
        query_stack_ref[p] = pair_stack(queries[:, pair]).T
        cot_stack_ref[p] = pair_stack(cot_ref[:, pair]).T
    key_ref[...] = dot(own_ref[...], wk_ref[...]).astype(jnp.bfloat16)
    value_ref[...] = dot(own_ref[...], wv_ref[...]).astype(jnp.bfloat16)
    wqt_ref[...] = wq_ref[...].T
    wkt_ref[...] = wk_ref[...].T
    wvt_ref[...] = wv_ref[...].T


def step_entry(work_ref, index):
    at = 1 + 2 * TILES * index
    return [work_ref[at + 2 * t] for t in range(TILES)], [work_ref[at + 2 * t + 1] for t in range(TILES)]


def run_steps(work_ref, start, wait, body):
    total = work_ref[0]

    def step(index, carry):
        @pl.when(index + 1 < total)
        def _():
            start(lax.rem(index + 1, 2), *step_entry(work_ref, index + 1))

        slot = lax.rem(index, 2)
        wait(slot)
        body(slot, *step_entry(work_ref, index), index)
        return carry

    lax.fori_loop(0, total, step, 0)


def first_step(work_ref, start):
    start(0, *step_entry(work_ref, 0))


class Rows:
    def __init__(self, layout, groups, mask_ref, buf, words, sems, block):
        self.layout, self.halves, self.mask_ref = layout, (groups[:4], groups[4:]), mask_ref
        self.buf, self.words, self.sems, self.block = buf, words, sems, block

    def rows(self, slot, t, k):
        half = self.block // 2
        into = self.buf.at[slot, pl.ds(t * self.block + k * half, half)]
        return lambda src: pltpu.make_async_copy(src.at[pl.ds(0, half)], into, self.sems.at[slot, t, k])

    def mask(self, slot, t, pattern):
        return pltpu.make_async_copy(self.mask_ref.at[pattern], self.words.at[slot, t], self.sems.at[slot, t, 2])

    def start(self, slot, blocks, patterns):
        for t in range(TILES):
            for k, order in enumerate(self.layout.orders()):
                start_copy(self.layout.row_place(order, blocks[t]), self.halves[k], self.rows(slot, t, k))
            self.mask(slot, t, jnp.maximum(patterns[t], 0)).start()

    def wait(self, slot):
        for t in range(TILES):
            for k in range(2):
                self.rows(slot, t, k)(self.halves[k][0].at[0]).wait()
            self.mask(slot, t, 0).wait()

    def bias(self, slot, blocks, patterns):
        parts = [
            tile_bias(self.words[slot, t], patterns[t], blocks[t] == self.layout.me) for t in range(TILES)
        ]
        return jnp.concatenate(parts, 0)


def forward_kernel(sizes, work_ref, stack_ref, cot_ref, wk_ref, wvt_ref, mask_ref, *refs):
    groups, refs = refs[:8], refs[8:]
    out_ref, sent_ref, stats_ref, buf, words, bias_ref, max_ref, sum_ref, acc_ref, score_ref, sems = refs
    layout = Layout(*sizes)
    block, width = cot_ref.shape
    head = width // HEADS
    rows_in = Rows(layout, groups, mask_ref, buf, words, sems, block)
    first_step(work_ref, rows_in.start)
    max_ref[...] = jnp.full(max_ref.shape, NEG_FILL, jnp.float32)
    sum_ref[...] = jnp.zeros(sum_ref.shape, jnp.float32)
    acc_ref[...] = jnp.zeros(acc_ref.shape, jnp.float32)

    def tiles(slot, blocks, patterns, index):
        rows = buf[slot]
        keys = dot(rows, wk_ref[...]).astype(jnp.bfloat16)
        values = dot(wvt_ref[...], rows, NT).astype(jnp.bfloat16)
        bias_ref[...] = rows_in.bias(slot, blocks, patterns)
        for p in range(HEADS // 2):
            scores = dot(keys[:, 2 * head * p : 2 * head * (p + 1)], stack_ref[p])
            for e in range(2):
                score_ref[2 * p + e] = scores[:, block * e : block * (e + 1)] + bias_ref[...]
        for h in range(HEADS):
            s = score_ref[h]
            old = max_ref[h : h + 1]
            new = jnp.maximum(old, jnp.max(s, axis=0, keepdims=True))
            fade = jnp.exp(old - new)
            expo = jnp.exp(s - new)
            max_ref[h : h + 1] = new
            sum_ref[h : h + 1] = sum_ref[h : h + 1] * fade + jnp.sum(expo, axis=0, keepdims=True)
            at = slice(head * h, head * (h + 1))
            acc_ref[at] = acc_ref[at] * fade + dot(values[at], expo.astype(jnp.bfloat16))

    run_steps(work_ref, rows_in.start, rows_in.wait, tiles)
    inverse = 1.0 / sum_ref[...]
    cot = cot_ref[...].astype(jnp.float32).T
    stats_ref[0:HEADS] = max_ref[...] + jnp.log(sum_ref[...])
    for h in range(HEADS):
        at = slice(head * h, head * (h + 1))
        outputs = acc_ref[at] * inverse[h : h + 1]
        acc_ref[at] = outputs
        stats_ref[HEADS + h : HEADS + h + 1] = jnp.sum(outputs * cot[at], axis=0, keepdims=True)
    sent_ref[...] = jnp.broadcast_to(stats_ref[...], sent_ref.shape)
    out_ref[...] = acc_ref[...].T.astype(out_ref.dtype)


def tile_grads(scores, d_probs, lse, delta):
    prob = jnp.exp(scores - lse)
    return prob.astype(jnp.bfloat16), (prob * (d_probs - delta)).astype(jnp.bfloat16)


def query_grad_kernel(
    sizes, work_ref, stack_hbm, cot_stack_hbm, stats_hbm, wqt_hbm, wk_hbm, wkt_hbm, wv_hbm, mask_ref, *refs
):
    groups, refs = refs[:8], refs[8:]
    part_ref, stack_ref, cot_stack_ref, stats_ref, wqt_ref, wk_ref, wkt_ref, wv_ref = refs[:8]
    buf, words, bias_ref, acc_ref, score_ref, d_prob_ref, sems, w_sems = refs[8:]
    layout = Layout(*sizes)
    block, width = part_ref.shape
    head = width // HEADS
    rows_in = Rows(layout, groups, mask_ref, buf, words, sems, block)
    first_step(work_ref, rows_in.start)
    loads = load((
        (wk_hbm, wk_ref), (stack_hbm, stack_ref), (wv_hbm, wv_ref), (cot_stack_hbm, cot_stack_ref),
        (wkt_hbm, wkt_ref), (stats_hbm.at[0], stats_ref), (wqt_hbm, wqt_ref),
    ), w_sems)
    acc_ref[...] = jnp.zeros(acc_ref.shape, jnp.float32)
    for copy in loads[:6]:
        copy.wait()

    def tiles(slot, blocks, patterns, index):
        rows = buf[slot]
        keys = dot(rows, wk_ref[...]).astype(jnp.bfloat16)
        values = dot(rows, wv_ref[...]).astype(jnp.bfloat16)
        keys_t = dot(wkt_ref[...], rows, NT).astype(jnp.bfloat16)
        bias_ref[...] = rows_in.bias(slot, blocks, patterns)
        for p in range(HEADS // 2):
            pair = slice(2 * head * p, 2 * head * (p + 1))
            scores = dot(keys[:, pair], stack_ref[p])
            d_probs = dot(values[:, pair], cot_stack_ref[p])
            for e in range(2):
                of = slice(block * e, block * (e + 1))
                score_ref[2 * p + e] = scores[:, of] + bias_ref[...]
                d_prob_ref[2 * p + e] = d_probs[:, of]
        for h in range(HEADS):
            _, d_scores = tile_grads(
                score_ref[h], d_prob_ref[h], stats_ref[h : h + 1], stats_ref[HEADS + h : HEADS + h + 1]
            )
            at = slice(head * h, head * (h + 1))
            acc_ref[at] += dot(keys_t[at], d_scores)

    run_steps(work_ref, rows_in.start, rows_in.wait, tiles)
    loads[6].wait()
    grad = (acc_ref[...].T * (head**-0.5)).astype(jnp.bfloat16)
    part_ref[...] = dot(grad, wqt_ref[...])


def key_grad_kernel(
    sizes, bits, work_ref, key_hbm, value_hbm, wq_hbm, wkt_hbm, wvt_hbm, part_hbm, mask_ref, stats_all_ref, *refs
):
    readers = sizes[0]
    groups, refs = refs[:8], refs[8:]
    halves, refs = (refs[:readers], refs[readers : 2 * readers]), refs[2 * readers :]
    out_ref, key_ref, value_ref, part_ref, wq_ref, wkt_ref, wvt_ref, buf, words, cot_buf, stats, bias_ref = refs[:12]
    query_stack_ref, cot_stack_ref, score_ref, d_prob_ref, key_acc, value_acc, sems, c_sems, w_sems = refs[12:]
    layout = Layout(*sizes)
    block, width = out_ref.shape
    head = width // HEADS
    rows_in = Rows(layout, groups, mask_ref, buf, words, sems, block)

    def half_copy(slot, t, k):
        into = cot_buf.at[slot, pl.ds(t * block + block // 2 * k, block // 2)]
        return lambda src: pltpu.make_async_copy(src, into, c_sems.at[slot, t, k])

    def stats_copy(slot, t, query):
        return pltpu.make_async_copy(stats_all_ref.at[query], stats.at[slot, t], c_sems.at[slot, t, 2])

    def start(slot, blocks, patterns):
        rows_in.start(slot, blocks, patterns)
        for t in range(TILES):
            stats_copy(slot, t, blocks[t]).start()
            for k in range(2):
                start_copy(layout.half_place(bits[k], blocks[t]), halves[k], half_copy(slot, t, k))

    def wait(slot):
        rows_in.wait(slot)
        for t in range(TILES):
            stats_copy(slot, t, 0).wait()
            for k in range(2):
                half_copy(slot, t, k)(halves[k][0].at[0]).wait()

    first_step(work_ref, start)
    loads = load((
        (wq_hbm, wq_ref), (key_hbm, key_ref), (value_hbm, value_ref),
        (wkt_hbm, wkt_ref), (wvt_hbm, wvt_ref), (part_hbm, part_ref),
    ), w_sems)
    key_acc[...] = jnp.zeros(key_acc.shape, jnp.float32)
    value_acc[...] = jnp.zeros(value_acc.shape, jnp.float32)
    for copy in loads[:3]:
        copy.wait()

    def tiles(slot, blocks, patterns, index):
        queries = dot(buf[slot], wq_ref[...]).astype(jnp.bfloat16) * jnp.bfloat16(head**-0.5)
        bias_ref[...] = rows_in.bias(slot, blocks, patterns)
        cots = cot_buf[slot]
        pairs = [slice(2 * head * p, 2 * head * (p + 1)) for p in range(HEADS // 2)]
        of_tile = [slice(block * t, block * (t + 1)) for t in range(TILES)]
        for p, pair in enumerate(pairs):
            query_stack_ref[p] = jnp.concatenate([pair_stack(queries[of, pair]) for of in of_tile], 0)
            cot_stack_ref[p] = jnp.concatenate([pair_stack(cots[of, pair]) for of in of_tile], 0)
            score_ref[p] = dot(key_ref[:, pair], query_stack_ref[p], NT)
            d_prob_ref[p] = dot(value_ref[:, pair], cot_stack_ref[p], NT)
        for p, pair in enumerate(pairs):
            probs, d_scores = [], []
            for t in range(TILES):
                for e in range(2):
                    h = 2 * p + e
                    of = slice(block * (2 * t + e), block * (2 * t + e + 1))
                    prob, d_score = tile_grads(
                        score_ref[p, :, of] + bias_ref[of_tile[t]], d_prob_ref[p, :, of], stats[slot, t, h : h + 1],
                        stats[slot, t, HEADS + h : HEADS + h + 1],
                    )
                    probs.append(prob)
                    d_scores.append(d_score)
            value_acc[:, pair] += dot(jnp.concatenate(probs, 1), cot_stack_ref[p])
            key_acc[:, pair] += dot(jnp.concatenate(d_scores, 1), query_stack_ref[p])

    run_steps(work_ref, start, wait, tiles)
    for copy in loads[3:]:
        copy.wait()
    grad = part_ref[...] + dot(key_acc[...].astype(jnp.bfloat16), wkt_ref[...])
    grad = grad + dot(value_acc[...].astype(jnp.bfloat16), wvt_ref[...])
    out_ref[...] = grad.astype(out_ref.dtype)


VMEM = pl.BlockSpec(memory_space=pltpu.VMEM)
SMEM = pl.BlockSpec(memory_space=pltpu.SMEM)
HBM = pl.BlockSpec(memory_space=pltpu.HBM)


def swap(block, mask):
    axes = ("reader", "blk")
    count = lax.axis_size("reader") * lax.axis_size("blk")
    return lax.ppermute(block, axes, [(i, i ^ mask) for i in range(count)])


def after(value, *others):
    return lax.optimization_barrier((value, *others))[0]


def over_readers(chunk, order, blks):
    for bit in order[:-1]:
        chunk = jnp.concatenate([chunk, swap(chunk, blks << bit)], 0)
    return [chunk, swap(chunk, blks << order[-1])]


def local(features, cotangent, w_query, w_key, w_value, tile_coords, tile_count, mask_table):
    block, width = features.shape
    readers, blks, cap = lax.axis_size("reader"), lax.axis_size("blk"), tile_coords.shape[2]
    assert block == mask_table.shape[1] and 3 * cap < 128
    sizes = (readers, blks, cap)
    devices, lines = readers * blks, blks // 2
    f32, bf16, i32 = jnp.float32, jnp.bfloat16, jnp.int32
    shape = jax.ShapeDtypeStruct
    masks = mask_table.transpose(0, 2, 1)
    words = masks.shape[1]
    head = width // HEADS
    half = block // 2
    some = pltpu.CompilerParams(vmem_limit_bytes=VMEM_SOME)
    most = pltpu.CompilerParams(vmem_limit_bytes=VMEM_MOST)
    axes = ("reader", "blk")

    def cost(tiles):
        return pl.CostEstimate(flops=tiles * 200_000_000, bytes_accessed=4_000_000, transcendentals=tiles * 131072)

    packed = pl.pallas_call(
        pack_kernel,
        out_shape=shape((1, block + LIST_ROWS, width), bf16),
        in_specs=[HBM, HBM, HBM],
        out_specs=VMEM,
        scratch_shapes=[
            pltpu.SMEM((1, 3, 1, cap), i32), pltpu.SMEM((1, 1), i32), pltpu.SemaphoreType.DMA((3,)),
        ],
        compiler_params=most,
        name="pack",
    )(features, tile_coords.transpose(0, 3, 1, 2), tile_count)
    lined = [packed] + [swap(packed, 2 * k) for k in range(1, lines)]

    bits = (0, (readers - 1).bit_length() - 1)
    cot_parts = [
        jnp.concatenate([cotangent[None, half * k : half * (k + 1)], packed[:, block:]], 1) for k in range(2)
    ]
    cot_other = [swap(part, blks << bit) for part, bit in zip(cot_parts, bits)]

    own_list = packed[:, block:, :128]
    columns = {1 << bit: other[:, half:, :128] for bit, other in zip(bits, cot_other)}
    line_lists = jnp.concatenate([entry[:, block:, :128] for entry in lined], 0)
    row_lists = jnp.concatenate([line_lists, swap(line_lists, 1)], 0)
    far_list = after(own_list, row_lists)
    columns = {k: columns[k] if k in columns else swap(far_list, blks * k) for k in range(1, readers)}
    column_lists = jnp.concatenate([own_list] + [columns[k] for k in range(1, readers)], 0)

    def work(kernel, lists, count, name):
        return pl.pallas_call(
            functools.partial(kernel, sizes),
            out_shape=shape((2 * count * cap + 5,), i32),
            in_specs=[HBM],
            out_specs=SMEM,
            scratch_shapes=[pltpu.SMEM((count, 128), i32), pltpu.SemaphoreType.DMA],
            compiler_params=some,
            cost_estimate=cost(1),
            name=name,
        )(lists[:, 0].astype(i32))

    query_work = work(query_work_kernel, row_lists, blks, "query_work")
    key_work = work(key_work_kernel, column_lists, readers, "key_work")

    stacks = shape((HEADS // 2, 2 * head, 2 * block), bf16)
    own = shape((block, width), bf16)
    square = shape((width, width), bf16)
    weight = pltpu.VMEM((width, width), bf16)
    rows_low, rows_wide = pltpu.VMEM((block, width), bf16), pltpu.VMEM((block, width), f32)
    prepared = pl.pallas_call(
        prepare_kernel,
        out_shape=(stacks, stacks, own, own, square, square, square),
        in_specs=[HBM] * 5,
        out_specs=(VMEM,) * 7,
        scratch_shapes=[rows_low, rows_low, weight, weight, weight, pltpu.SemaphoreType.DMA((5,))],
        compiler_params=most,
        cost_estimate=cost(2),
        name="prepare",
    )(features, cotangent, w_query, w_key, w_value)
    query_stack, cot_stack, keys, values, w_query_t, w_key_t, w_value_t = prepared

    lined = after(lined, prepared)
    chunks = [jnp.concatenate([entry[:, half * k : half * (k + 1)] for entry in lined], 0) for k in range(2)]
    here = [over_readers(chunk, order, blks) for chunk, order in zip(chunks, orders(readers))]
    rows_all = []
    for first, last in here:
        rows_all += [first, last, swap(first, 1), swap(last, 1)]

    pairs = [part[:, :half] for k in range(2) for part in (cot_parts[k], cot_other[k])]
    pieces = [after(jnp.concatenate(pairs, 0), *chunks, row_lists)]
    mask = blks // 2
    while mask > 1:
        pieces += [swap(after(piece, query_work, key_work) if at else piece, mask) for at, piece in enumerate(pieces)]
        mask //= 2

    cots_here = []
    for k in range(2):
        part = jnp.concatenate([piece[2 * k : 2 * k + 2] for piece in pieces], 0)
        masks_left = [m for m in range(1, readers) if not m >> bits[k] & 1]
        cots_here.append((part, [swap(after(part, here), blks * m) for m in masks_left]))

    stack_space = pltpu.VMEM(stacks.shape, bf16)
    buffer = pltpu.VMEM((2, TILES * block, width), bf16)
    word_buffer = pltpu.VMEM((2, TILES, words, block), i32)
    bias = pltpu.VMEM((TILES * block, block), f32)
    turned = pltpu.VMEM((width, block), f32)
    per_head = pltpu.VMEM((HEADS, block), f32)
    own_stats = pltpu.VMEM((2 * HEADS, block), f32)
    met = pltpu.VMEM((HEADS, TILES * block, block), f32)
    pair_met = pltpu.VMEM((HEADS // 2, block, 2 * TILES * block), f32)
    pair_rows = pltpu.VMEM((HEADS // 2, 2 * TILES * block, 2 * head), bf16)
    row_sems = pltpu.SemaphoreType.DMA((2, TILES, 3))

    attn_out, stats = pl.pallas_call(
        functools.partial(forward_kernel, sizes),
        out_shape=(own, shape((devices, 2 * HEADS, block), f32)),
        in_specs=[SMEM] + [VMEM] * 4 + [HBM] * 9,
        out_specs=(VMEM, VMEM),
        scratch_shapes=[own_stats, buffer, word_buffer, bias, per_head, per_head, turned, met, row_sems],
        compiler_params=some,
        cost_estimate=cost(5),
        name="forward",
    )(query_work, query_stack, cotangent, w_key, w_value_t, masks, *rows_all)

    stats_all = lax.all_to_all(stats, axes, 0, 0, tiled=True)

    query_part = pl.pallas_call(
        functools.partial(query_grad_kernel, sizes),
        out_shape=shape((block, width), f32),
        in_specs=[SMEM] + [HBM] * 16,
        out_specs=VMEM,
        scratch_shapes=[
            stack_space, stack_space, own_stats, weight, weight, weight, weight, buffer, word_buffer, bias, turned,
            met, met, row_sems, pltpu.SemaphoreType.DMA((7,)),
        ],
        compiler_params=most,
        cost_estimate=cost(5),
        name="query_grad",
    )(query_work, query_stack, cot_stack, stats, w_query_t, w_key, w_key_t, w_value, masks, *rows_all)

    cots_all = []
    for first, rest in cots_here:
        cots_all += [first, *rest, swap(after(first, stats), 1)]
        cots_all += [swap(after(part, stats_all, query_part), 1) for part in rest]

    grad_features = pl.pallas_call(
        functools.partial(key_grad_kernel, sizes, bits),
        out_shape=own,
        in_specs=[SMEM] + [HBM] * (16 + 2 * readers),
        out_specs=VMEM,
        scratch_shapes=[
            rows_low, rows_low, rows_wide, weight, weight, weight,
            buffer, word_buffer, buffer, pltpu.VMEM((2, TILES, 2 * HEADS, block), f32), bias,
            pair_rows, pair_rows, pair_met, pair_met, rows_wide, rows_wide,
            row_sems, pltpu.SemaphoreType.DMA((2, TILES, 3)), pltpu.SemaphoreType.DMA((6,)),
        ],
        compiler_params=most,
        cost_estimate=cost(5),
        name="key_grad",
    )(key_work, keys, values, w_query, w_key_t, w_value_t, query_part, masks, stats_all, *rows_all, *cots_all)
    return attn_out, grad_features


def solution(mesh):
    return jax.shard_map(
        local,
        mesh=mesh,
        in_specs=(
            P(("reader", "blk"), None),
            P(("reader", "blk"), None),
            P(),
            P(),
            P(),
            P("reader", "blk", None, None),
            P("reader", "blk"),
            P(),
        ),
        out_specs=(P(("reader", "blk"), None), P(("reader", "blk"), None)),
        check_vma=False,
    )
```

profile of v0, /device:TPU:0, one launch (start us, length us, event | category | flops | bytes accessed | tf_op | source)
XLA Modules:
  0.0 77.5 jit_solution(13101245494636722065)
XLA Ops:
  1.3 0.0 copy-start.11
  1.3 1.6 %pack.1 = bf16[1,144,512]{2,1,0:T(8,128)(2,1)} custom-call(bf16[128,512]{1,0:T(8,128)(2,1)} %own_hbm.3, s32[1,3,1,8]{3,2,1,0:T(1,128)} %bitcast.13, s32[1,1]{1,0:T(1,128)S(6)} %copy.22.count_hbm), custom_call_target="tpu_custom_call" | custom-call | tf_op jit(solution)/shard_map/pack/pallas_call | solution.py:456
  2.9 5.1 %collective-permute-start.2 = (bf16[1,144,512]{2,1,0:T(8,128)(2,1)}, bf16[1,144,512]{2,1,0:T(8,128)(2,1)S(1)}, u32[]{:S(2)}, u32[]{:S(2)}) collective-permute-start(bf16[1,144,512]{2,1,0:T(8,128)(2,1)} %pack.1), channel_id=1, source_target_pairs={{0,6},{1,7},{2,4},{3,5},{4,2},{5,3},{6,0},{7,1},{8,14},{9,15},{10,... | collective-permute-start | bytes 442376 | tf_op jit(solution)/shard_map/ppermute | solution.py:424
  8.0 0.0 collective-permute-start.1
  8.0 0.6 collective-permute-start
  8.7 0.8 slice.123
  9.5 1.7 %collective-permute-start.12 = (bf16[1,80,512]{2,1,0:T(8,128)(2,1)S(1)}, bf16[1,80,512]{2,1,0:T(8,128)(2,1)S(1)}, u32[]{:S(2)}, u32[]{:S(2)}) collective-permute-start(bf16[1,80,512]{2,1,0:T(8,128)(2,1)S(1)} %get-tuple-element.80), channel_id=1, source_target_pairs={{0,8},{1,9},{2,10},{3,11},{4,12},{5,13},{6,14},{7,15},{8,0},{9,1},... | collective-permute-start | bytes 245768 | tf_op jit(solution)/shard_map/ppermute | solution.py:424
  11.2 1.5 %collective-permute-start.13 = (bf16[1,80,512]{2,1,0:T(8,128)(2,1)S(1)}, bf16[1,80,512]{2,1,0:T(8,128)(2,1)S(1)}, u32[]{:S(2)}, u32[]{:S(2)}) collective-permute-start(bf16[1,80,512]{2,1,0:T(8,128)(2,1)S(1)} %get-tuple-element.81), channel_id=1, source_target_pairs={{0,16},{1,17},{2,18},{3,19},{4,20},{5,21},{6,22},{7,23},{8,24},{9,... | collective-permute-start | bytes 245768 | tf_op jit(solution)/shard_map/ppermute | solution.py:424
  12.7 3.3 %prepare.1 = (bf16[4,128,256]{2,1,0:T(8,128)(2,1)}, bf16[4,128,256]{2,1,0:T(8,128)(2,1)}, bf16[128,512]{1,0:T(8,128)(2,1)}, bf16[128,512]{1,0:T(8,128)(2,1)}, bf...) custom-call(bf16[128,512]{1,0:T(8,128)(2,1)} %own_hbm.3, bf16[128,512]{1,0:T(8,128)(2,1)} %cot_ref.1, ...), custom_call_target="tpu_custom_call" | custom-call | flops 400000000 | bytes 4000000 | tf_op jit(solution)/shard_map/prepare/pallas_call | solution.py:503
  16.1 0.0 copy-start.25
  16.1 0.6 copy-done.25
  16.7 0.0 collective-permute-done.13
  16.7 0.8 %slice-done = bf16[1,64,512]{2,1,0:T(8,128)(2,1)S(1)} async-done(((bf16[1,80,512]{2,1,0:T(8,128)(2,1)}), bf16[1,64,512]{2,1,0:T(8,128)(2,1)S(1)}, s32[]{:S(2)}) %slice-start) | async-done | bytes 65560 | tf_op jit(solution)/shard_map/slice | solution.py:522
  17.6 0.3 collective-permute-done
  17.9 2.9 %collective-permute-done.1 = bf16[1,144,512]{2,1,0:T(8,128)(2,1)S(1)} collective-permute-done((bf16[1,144,512]{2,1,0:T(8,128)(2,1)}, bf16[1,144,512]{2,1,0:T(8,128)(2,1)S(1)}, u32[]{:S(2)}, u32[]{:S(2)}) %collective-permute-start.1) | collective-permute-done | bytes 147488 | tf_op jit(solution)/shard_map/ppermute | solution.py:424
  20.8 0.1 collective-permute-start.3
  21.0 1.6 %collective-permute-start.4 = (bf16[4,64,512]{2,1,0:T(8,128)(2,1)S(1)}, bf16[4,64,512]{2,1,0:T(8,128)(2,1)S(1)}, u32[]{:S(2)}, u32[]{:S(2)}) collective-permute-start(bf16[4,64,512]{2,1,0:T(8,128)(2,1)S(1)} %pad_maximum_fusion.2), channel_id=1, source_target_pairs={{0,8},{1,9},{2,10},{3,11},{4,12},{5,13},{6,14},{7,15},{8,0},{9,1},... | collective-permute-start | bytes 786440 | tf_op jit(solution)/shard_map/ppermute | solution.py:424
  22.6 1.6 %collective-permute-start.8 = (bf16[4,64,512]{2,1,0:T(8,128)(2,1)S(1)}, bf16[4,64,512]{2,1,0:T(8,128)(2,1)S(1)}, u32[]{:S(2)}, u32[]{:S(2)}) collective-permute-start(bf16[4,64,512]{2,1,0:T(8,128)(2,1)S(1)} %pad_maximum_fusion.3), channel_id=1, source_target_pairs={{0,16},{1,17},{2,18},{3,19},{4,20},{5,21},{6,22},{7,23},{8,24},{9,... | collective-permute-start | bytes 786440 | tf_op jit(solution)/shard_map/ppermute | solution.py:424
  24.2 0.0 collective-permute-done.3
  24.2 0.0 collective-permute-start.16
  24.2 3.1 %collective-permute-start.15 = (bf16[4,64,512]{2,1,0:T(8,128)(2,1)S(1)}, bf16[4,64,512]{2,1,0:T(8,128)(2,1)S(1)}, u32[]{:S(2)}, u32[]{:S(2)}) collective-permute-start(bf16[4,64,512]{2,1,0:T(8,128)(2,1)S(1)} %pad_maximum_fusion.4), channel_id=1, source_target_pairs={{0,4},{1,5},{2,6},{3,7},{4,0},{5,1},{6,2},{7,3},{8,12},{9,13},{10,... | collective-permute-start | bytes 786440 | tf_op jit(solution)/shard_map/ppermute | solution.py:424
  27.3 0.5 collective-permute-start.14
  27.8 3.4 %collective-permute-done.8 = bf16[4,64,512]{2,1,0:T(8,128)(2,1)S(1)} collective-permute-done((bf16[4,64,512]{2,1,0:T(8,128)(2,1)S(1)}, bf16[4,64,512]{2,1,0:T(8,128)(2,1)S(1)}, u32[]{:S(2)}, u32[]{:S(2)}) %collective-permute-start.8) | collective-permute-done | bytes 262176 | tf_op jit(solution)/shard_map/ppermute | solution.py:424
  31.1 0.6 collective-permute-start.9
  31.7 0.0 collective-permute-done.4
  31.7 1.7 %collective-permute-start.5 = (bf16[8,64,512]{2,1,0:T(8,128)(2,1)S(1)}, bf16[8,64,512]{2,1,0:T(8,128)(2,1)S(1)}, u32[]{:S(2)}, u32[]{:S(2)}) collective-permute-start(bf16[8,64,512]{2,1,0:T(8,128)(2,1)S(1)} %constant_dynamic-update-slice_fusion.5.refs_0_), channel_id=1, source_target_pairs={{0,16},{1,17},{2,18},{3,19},{4,20},{5,21},{6,22},{7,23},{8,24},{9,... | collective-permute-start | bytes 1572872 | tf_op jit(solution)/shard_map/ppermute | solution.py:424
  33.4 1.6 %query_work.1.work_ref = s32[133]{0:T(256)S(1)} custom-call(s32[8,128]{1,0:T(8,128)S(1)} %bitcast.11), custom_call_target="tpu_custom_call" | custom-call | flops 200000000 | bytes 4000000 | tf_op jit(solution)/shard_map/query_work/pallas_call | solution.py:484
  35.1 0.0 copy-start.14
  35.1 1.4 %key_work.1.work_ref = s32[69]{0:T(128)S(1)} custom-call(s32[4,128]{1,0:T(4,128)S(1)} %bitcast.12), custom_call_target="tpu_custom_call" | custom-call | flops 200000000 | bytes 4000000 | tf_op jit(solution)/shard_map/key_work/pallas_call | solution.py:484
  36.5 0.5 copy-done.15
  37.0 0.0 collective-permute-start.10
  37.0 2.0 %collective-permute-done.15 = bf16[4,64,512]{2,1,0:T(8,128)(2,1)S(1)} collective-permute-done((bf16[4,64,512]{2,1,0:T(8,128)(2,1)S(1)}, bf16[4,64,512]{2,1,0:T(8,128)(2,1)S(1)}, u32[]{:S(2)}, u32[]{:S(2)}) %collective-permute-start.15) | collective-permute-done | bytes 262176 | tf_op jit(solution)/shard_map/ppermute | solution.py:424
  39.0 0.3 collective-permute-start.17
  39.4 0.0 collective-permute-done.16
  39.4 0.1 collective-permute-start.6
  39.5 4.9 %collective-permute-done.9.refs_5_ = bf16[8,64,512]{2,1,0:T(8,128)(2,1)S(1)} collective-permute-done((bf16[8,64,512]{2,1,0:T(8,128)(2,1)S(1)}, bf16[8,64,512]{2,1,0:T(8,128)(2,1)S(1)}, u32[]{:S(2)}, u32[]{:S(2)}) %collective-permute-start.9) | collective-permute-done | bytes 524320 | tf_op jit(solution)/shard_map/ppermute | solution.py:424
  44.4 0.0 collective-permute-start.11
  44.4 0.3 collective-permute-done.5.refs_1_
  44.7 0.2 collective-permute-start.7
  45.0 0.8 %collective-permute-done.17 = bf16[4,64,512]{2,1,0:T(8,128)(2,1)S(1)} collective-permute-done((bf16[4,64,512]{2,1,0:T(8,128)(2,1)S(1)}, bf16[4,64,512]{2,1,0:T(8,128)(2,1)S(1)}, u32[]{:S(2)}, u32[]{:S(2)}) %collective-permute-start.17) | collective-permute-done | bytes 262176 | tf_op jit(solution)/shard_map/ppermute | solution.py:424
  45.8 0.0 copy-start.12
  45.8 0.1 pad_maximum_fusion.1.refs_12_
  45.9 0.0 copy-start.2
  45.9 0.0 copy-start.9
  45.9 0.1 pad_maximum_fusion.refs_8_
  46.0 0.8 %collective-permute-start.18 = (bf16[8,64,512]{2,1,0:T(8,128)(2,1)S(1)}, bf16[8,64,512]{2,1,0:T(8,128)(2,1)S(1)}, u32[]{:S(2)}, u32[]{:S(2)}) collective-permute-start(bf16[8,64,512]{2,1,0:T(8,128)(2,1)S(1)} %pad_maximum_fusion.refs_8_), channel_id=1, source_target_pairs={{0,16},{1,17},{2,18},{3,19},{4,20},{5,21},{6,22},{7,23},{8,24},{9,... | collective-permute-start | bytes 1572872 | tf_op jit(solution)/shard_map/ppermute | solution.py:424
  46.8 0.0 collective-permute-done.10.refs_6_
  46.8 1.3 %collective-permute-start.21 = (bf16[8,64,512]{2,1,0:T(8,128)(2,1)S(1)}, bf16[8,64,512]{2,1,0:T(8,128)(2,1)S(1)}, u32[]{:S(2)}, u32[]{:S(2)}) collective-permute-start(bf16[8,64,512]{2,1,0:T(8,128)(2,1)S(1)} %pad_maximum_fusion.1.refs_12_), channel_id=1, source_target_pairs={{0,8},{1,9},{2,10},{3,11},{4,12},{5,13},{6,14},{7,15},{8,0},{9,1},... | collective-permute-start | bytes 1572872 | tf_op jit(solution)/shard_map/ppermute | solution.py:424
  48.2 0.0 collective-permute-done.6.refs_2_
  48.2 0.0 collective-permute-done.11.refs_7_
  48.2 0.0 collective-permute-done.7.refs_3_
  48.3 2.9 %forward.1 = (bf16[128,512]{1,0:T(8,128)(2,1)}, f32[32,16,128]{2,1,0:T(8,128)}) custom-call(s32[133]{0:T(256)S(1)} %query_work.1.work_ref, bf16[4,128,256]{2,1,0:T(8,128)(2,1)S(1)} %copy-done.13, bf16[128,512]{1,0:T(8,128)(2,1)S(1)} %copy-done.12, bf16[512,512]{1,0:T(8,128)(2,1)S(1)} %copy-done.2, bf16[512,512]{1,0:T(8,128)(2,1)S(1)} %copy-done.10, ...), custom_call_target="tpu_custom_call" | custom-call | flops 1000000000 | bytes 4000000 | tf_op jit(solution)/shard_map/forward/pallas_call | solution.py:547
  51.3 6.7 %all-to-all-start = ((f32[32,16,128]{2,1,0:T(8,128)}), f32[32,16,128]{2,1,0:T(8,128)S(1)}, u32[]{:S(2)}, u32[]{:S(2)}) async-start(f32[32,16,128]{2,1,0:T(8,128)} %get-tuple-element.37.stats_hbm), calls=%async_computation | async-start | bytes 524288 | tf_op jit(solution)/shard_map/all_to_all | solution.py:558
  58.0 0.3 collective-permute-start.19
  58.3 0.3 collective-permute-start.22
  58.6 4.6 %query_grad.1.part_hbm = f32[128,512]{1,0:T(8,128)} custom-call(s32[133]{0:T(256)} %copy-done.14, bf16[4,128,256]{2,1,0:T(8,128)(2,1)} %get-tuple-element.24.stack_ref.stack_hbm, bf16[4,128,256]{2,1,0:T(8,128)(2,1)} %get-tuple-element.26.cot_stack_hbm, f32[32,16,128]{2,1,0:T(8,128)} %get-tuple-element.37.stats_hbm, ...), custom_call_target="tpu_custom_call" | custom-call | flops 1000000000 | bytes 4000000 | tf_op jit(solution)/shard_map/query_grad/pallas_call | solution.py:560
  63.1 5.2 %all-to-all-done.stats_all_ref = f32[32,16,128]{2,1,0:T(8,128)S(1)} async-done(((f32[32,16,128]{2,1,0:T(8,128)}), f32[32,16,128]{2,1,0:T(8,128)S(1)}, u32[]{:S(2)}, u32[]{:S(2)}) %all-to-all-start) | async-done | bytes 262176 | tf_op jit(solution)/shard_map/all_to_all | solution.py:558
  68.4 0.4 collective-permute-start.20
  68.8 0.1 collective-permute-start.23
  69.0 1.4 %collective-permute-done.20.refs_11_ = bf16[8,64,512]{2,1,0:T(8,128)(2,1)S(1)} collective-permute-done((bf16[8,64,512]{2,1,0:T(8,128)(2,1)S(1)}, bf16[8,64,512]{2,1,0:T(8,128)(2,1)S(1)}, u32[]{:S(2)}, u32[]{:S(2)}) %collective-permute-start.20) | collective-permute-done | bytes 524320 | tf_op jit(solution)/shard_map/ppermute | solution.py:424
  70.4 0.7 collective-permute-done.23.refs_15_
  71.1 0.0 copy-done.23
  71.1 0.8 %copy-done.24 = bf16[8,64,512]{2,1,0:T(8,128)(2,1)} copy-done((bf16[8,64,512]{2,1,0:T(8,128)(2,1)}, bf16[8,64,512]{2,1,0:T(8,128)(2,1)S(1)}, u32[]{:S(2)}) %copy-start.24) | copy-done | bytes 524312
  71.9 5.6 %key_grad.1 = bf16[128,512]{1,0:T(8,128)(2,1)} custom-call(s32[69]{0:T(128)} %copy-done.15, bf16[128,512]{1,0:T(8,128)(2,1)} %get-tuple-element.27.key_hbm, bf16[128,512]{1,0:T(8,128)(2,1)} %get-tuple-element.28.value_hbm, bf16[512,512]{1,0:T(8,128)(2,1)} %wq_hbm.3, bf16[512,512]{1,0:T(8,128)(2,1)} %get-tuple-element.30.wkt_hbm, ...), custom_call_target="tpu_custom_call" | custom-call | flops 1000000000 | bytes 4000000 | tf_op jit(solution)/shard_map/key_grad/pallas_call | solution.py:579
  (76 shorter events, 0.5 us)
Async XLA Ops:
  1.3 8.2 %copy-start.11 = (bf16[128,512]{1,0:T(8,128)(2,1)S(1)}, bf16[128,512]{1,0:T(8,128)(2,1)}, u32[]{:S(2)}) copy-start(bf16[128,512]{1,0:T(8,128)(2,1)} %cot_ref.1) | copy-start | bytes 393220
  2.9 17.8 %collective-permute-start.2 = (bf16[1,144,512]{2,1,0:T(8,128)(2,1)}, bf16[1,144,512]{2,1,0:T(8,128)(2,1)S(1)}, u32[]{:S(2)}, u32[]{:S(2)}) collective-permute-start(bf16[1,144,512]{2,1,0:T(8,128)(2,1)} %pack.1), channel_id=1, source_target_pairs={{0,6},{1,7},{2,4},{3,5},{4,2},{5,3},{6,0},{7,1},{8,14},{9,15},{10,... | collective-permute-start | bytes 442376 | tf_op jit(solution)/shard_map/ppermute | solution.py:424
  8.0 12.7 %collective-permute-start.1 = (bf16[1,144,512]{2,1,0:T(8,128)(2,1)}, bf16[1,144,512]{2,1,0:T(8,128)(2,1)S(1)}, u32[]{:S(2)}, u32[]{:S(2)}) collective-permute-start(bf16[1,144,512]{2,1,0:T(8,128)(2,1)} %pack.1), channel_id=1, source_target_pairs={{0,4},{1,5},{2,6},{3,7},{4,0},{5,1},{6,2},{7,3},{8,12},{9,13},{10,... | collective-permute-start | bytes 442376 | tf_op jit(solution)/shard_map/ppermute | solution.py:424
  8.0 9.8 %collective-permute-start = (bf16[1,144,512]{2,1,0:T(8,128)(2,1)}, bf16[1,144,512]{2,1,0:T(8,128)(2,1)S(1)}, u32[]{:S(2)}, u32[]{:S(2)}) collective-permute-start(bf16[1,144,512]{2,1,0:T(8,128)(2,1)} %pack.1), channel_id=1, source_target_pairs={{0,2},{1,3},{2,0},{3,1},{4,6},{5,7},{6,4},{7,5},{8,10},{9,11},{10,... | collective-permute-start | bytes 442376 | tf_op jit(solution)/shard_map/ppermute | solution.py:424
  9.4 3.3 %copy-start.19 = (bf16[1,144,512]{2,1,0:T(8,128)(2,1)S(1)}, bf16[1,144,512]{2,1,0:T(8,128)(2,1)}, u32[]{:S(2)}) copy-start(bf16[1,144,512]{2,1,0:T(8,128)(2,1)} %pack.1) | copy-start | bytes 442372
  9.5 6.6 %collective-permute-start.12 = (bf16[1,80,512]{2,1,0:T(8,128)(2,1)S(1)}, bf16[1,80,512]{2,1,0:T(8,128)(2,1)S(1)}, u32[]{:S(2)}, u32[]{:S(2)}) collective-permute-start(bf16[1,80,512]{2,1,0:T(8,128)(2,1)S(1)} %get-tuple-element.80), channel_id=1, source_target_pairs={{0,8},{1,9},{2,10},{3,11},{4,12},{5,13},{6,14},{7,15},{8,0},{9,1},... | collective-permute-start | bytes 245768 | tf_op jit(solution)/shard_map/ppermute | solution.py:424
  11.2 5.5 %collective-permute-start.13 = (bf16[1,80,512]{2,1,0:T(8,128)(2,1)S(1)}, bf16[1,80,512]{2,1,0:T(8,128)(2,1)S(1)}, u32[]{:S(2)}, u32[]{:S(2)}) collective-permute-start(bf16[1,80,512]{2,1,0:T(8,128)(2,1)S(1)} %get-tuple-element.81), channel_id=1, source_target_pairs={{0,16},{1,17},{2,18},{3,19},{4,20},{5,21},{6,22},{7,23},{8,24},{9,... | collective-permute-start | bytes 245768 | tf_op jit(solution)/shard_map/ppermute | solution.py:424
  16.1 0.6 copy-start.25
  16.7 0.8 %slice-start = ((bf16[1,80,512]{2,1,0:T(8,128)(2,1)}), bf16[1,64,512]{2,1,0:T(8,128)(2,1)S(1)}, s32[]{:S(2)}) async-start(bf16[1,80,512]{2,1,0:T(8,128)(2,1)} %copy-done.25), calls=%async_computation.1 | async-start | bytes 131072 | tf_op jit(solution)/shard_map/slice | solution.py:522
  20.8 3.4 %collective-permute-start.3 = (bf16[4,16,128]{2,1,0:T(8,128)(2,1)S(1)}, bf16[4,16,128]{2,1,0:T(8,128)(2,1)S(1)}, u32[]{:S(2)}, u32[]{:S(2)}) collective-permute-start(bf16[4,16,128]{2,1,0:T(8,128)(2,1)S(1)} %pad_maximum_fusion.7), channel_id=1, source_target_pairs={{0,1},{1,0},{2,3},{3,2},{4,5},{5,4},{6,7},{7,6},{8,9},{9,8},{10,11... | collective-permute-start | bytes 49160 | tf_op jit(solution)/shard_map/ppermute | solution.py:424
  21.0 10.7 %collective-permute-start.4 = (bf16[4,64,512]{2,1,0:T(8,128)(2,1)S(1)}, bf16[4,64,512]{2,1,0:T(8,128)(2,1)S(1)}, u32[]{:S(2)}, u32[]{:S(2)}) collective-permute-start(bf16[4,64,512]{2,1,0:T(8,128)(2,1)S(1)} %pad_maximum_fusion.2), channel_id=1, source_target_pairs={{0,8},{1,9},{2,10},{3,11},{4,12},{5,13},{6,14},{7,15},{8,0},{9,1},... | collective-permute-start | bytes 786440 | tf_op jit(solution)/shard_map/ppermute | solution.py:424
  22.6 8.5 %collective-permute-start.8 = (bf16[4,64,512]{2,1,0:T(8,128)(2,1)S(1)}, bf16[4,64,512]{2,1,0:T(8,128)(2,1)S(1)}, u32[]{:S(2)}, u32[]{:S(2)}) collective-permute-start(bf16[4,64,512]{2,1,0:T(8,128)(2,1)S(1)} %pad_maximum_fusion.3), channel_id=1, source_target_pairs={{0,16},{1,17},{2,18},{3,19},{4,20},{5,21},{6,22},{7,23},{8,24},{9,... | collective-permute-start | bytes 786440 | tf_op jit(solution)/shard_map/ppermute | solution.py:424
  24.2 15.2 %collective-permute-start.16 = (bf16[4,64,512]{2,1,0:T(8,128)(2,1)S(1)}, bf16[4,64,512]{2,1,0:T(8,128)(2,1)S(1)}, u32[]{:S(2)}, u32[]{:S(2)}) collective-permute-start(bf16[4,64,512]{2,1,0:T(8,128)(2,1)S(1)} %pad_maximum_fusion.4), channel_id=1, source_target_pairs={{0,2},{1,3},{2,0},{3,1},{4,6},{5,7},{6,4},{7,5},{8,10},{9,11},{10,... | collective-permute-start | bytes 786440 | tf_op jit(solution)/shard_map/ppermute | solution.py:424
  24.2 14.9 %collective-permute-start.15 = (bf16[4,64,512]{2,1,0:T(8,128)(2,1)S(1)}, bf16[4,64,512]{2,1,0:T(8,128)(2,1)S(1)}, u32[]{:S(2)}, u32[]{:S(2)}) collective-permute-start(bf16[4,64,512]{2,1,0:T(8,128)(2,1)S(1)} %pad_maximum_fusion.4), channel_id=1, source_target_pairs={{0,4},{1,5},{2,6},{3,7},{4,0},{5,1},{6,2},{7,3},{8,12},{9,13},{10,... | collective-permute-start | bytes 786440 | tf_op jit(solution)/shard_map/ppermute | solution.py:424
  27.3 7.8 %collective-permute-start.14 = (bf16[1,16,128]{2,1,0:T(8,128)(2,1)S(1)}, bf16[1,16,128]{2,1,0:T(8,128)(2,1)S(1)}, u32[]{:S(2)}, u32[]{:S(2)}) collective-permute-start(bf16[1,16,128]{2,1,0:T(8,128)(2,1)S(1)} %get-tuple-element.36), channel_id=1, source_target_pairs={{0,24},{1,25},{2,26},{3,27},{4,28},{5,29},{6,30},{7,31},{8,16},{9,... | collective-permute-start | bytes 12296 | tf_op jit(solution)/shard_map/ppermute | solution.py:424
  31.1 17.1 %copy-start.1 = (bf16[8,64,512]{2,1,0:T(8,128)(2,1)}, bf16[8,64,512]{2,1,0:T(8,128)(2,1)S(1)}, u32[]{:S(2)}) copy-start(bf16[8,64,512]{2,1,0:T(8,128)(2,1)S(1)} %constant_dynamic-update-slice_fusion.10.refs_4_) | copy-start | bytes 1572868
  31.1 13.3 %collective-permute-start.9 = (bf16[8,64,512]{2,1,0:T(8,128)(2,1)S(1)}, bf16[8,64,512]{2,1,0:T(8,128)(2,1)S(1)}, u32[]{:S(2)}, u32[]{:S(2)}) collective-permute-start(bf16[8,64,512]{2,1,0:T(8,128)(2,1)S(1)} %constant_dynamic-update-slice_fusion.10.refs_4_), channel_id=1, source_target_pairs={{0,8},{1,9},{2,10},{3,11},{4,12},{5,13},{6,14},{7,15},{8,0},{9,1},... | collective-permute-start | bytes 1572872 | tf_op jit(solution)/shard_map/ppermute | solution.py:424
  31.7 16.5 %copy-start = (bf16[8,64,512]{2,1,0:T(8,128)(2,1)}, bf16[8,64,512]{2,1,0:T(8,128)(2,1)S(1)}, u32[]{:S(2)}) copy-start(bf16[8,64,512]{2,1,0:T(8,128)(2,1)S(1)} %constant_dynamic-update-slice_fusion.5.refs_0_) | copy-start | bytes 1572868
  31.7 13.0 %collective-permute-start.5 = (bf16[8,64,512]{2,1,0:T(8,128)(2,1)S(1)}, bf16[8,64,512]{2,1,0:T(8,128)(2,1)S(1)}, u32[]{:S(2)}, u32[]{:S(2)}) collective-permute-start(bf16[8,64,512]{2,1,0:T(8,128)(2,1)S(1)} %constant_dynamic-update-slice_fusion.5.refs_0_), channel_id=1, source_target_pairs={{0,16},{1,17},{2,18},{3,19},{4,20},{5,21},{6,22},{7,23},{8,24},{9,... | collective-permute-start | bytes 1572872 | tf_op jit(solution)/shard_map/ppermute | solution.py:424
  35.1 13.2 %copy-start.14 = (s32[133]{0:T(256)}, s32[133]{0:T(256)S(1)}, u32[]{:S(2)}) copy-start(s32[133]{0:T(256)S(1)} %query_work.1.work_ref) | copy-start | bytes 1600
  36.5 0.5 copy-start.15
  37.0 9.8 %collective-permute-start.10 = (bf16[8,64,512]{2,1,0:T(8,128)(2,1)S(1)}, bf16[8,64,512]{2,1,0:T(8,128)(2,1)S(1)}, u32[]{:S(2)}, u32[]{:S(2)}) collective-permute-start(bf16[8,64,512]{2,1,0:T(8,128)(2,1)S(1)} %constant_dynamic-update-slice_fusion.10.refs_4_), channel_id=1, source_target_pairs={{0,1},{1,0},{2,3},{3,2},{4,5},{5,4},{6,7},{7,6},{8,9},{9,8},{10,11... | collective-permute-start | bytes 1572872 | tf_op jit(solution)/shard_map/ppermute | solution.py:424
  39.0 6.7 %collective-permute-start.17 = (bf16[4,64,512]{2,1,0:T(8,128)(2,1)S(1)}, bf16[4,64,512]{2,1,0:T(8,128)(2,1)S(1)}, u32[]{:S(2)}, u32[]{:S(2)}) collective-permute-start(bf16[4,64,512]{2,1,0:T(8,128)(2,1)S(1)} %collective-permute-done.15), channel_id=1, source_target_pairs={{0,2},{1,3},{2,0},{3,1},{4,6},{5,7},{6,4},{7,5},{8,10},{9,11},{10,... | collective-permute-start | bytes 786440 | tf_op jit(solution)/shard_map/ppermute | solution.py:424
  39.4 8.8 %collective-permute-start.6 = (bf16[8,64,512]{2,1,0:T(8,128)(2,1)S(1)}, bf16[8,64,512]{2,1,0:T(8,128)(2,1)S(1)}, u32[]{:S(2)}, u32[]{:S(2)}) collective-permute-start(bf16[8,64,512]{2,1,0:T(8,128)(2,1)S(1)} %constant_dynamic-update-slice_fusion.5.refs_0_), channel_id=1, source_target_pairs={{0,1},{1,0},{2,3},{3,2},{4,5},{5,4},{6,7},{7,6},{8,9},{9,8},{10,11... | collective-permute-start | bytes 1572872 | tf_op jit(solution)/shard_map/ppermute | solution.py:424
  44.4 3.8 %copy-start.3 = (bf16[8,64,512]{2,1,0:T(8,128)(2,1)}, bf16[8,64,512]{2,1,0:T(8,128)(2,1)S(1)}, u32[]{:S(2)}) copy-start(bf16[8,64,512]{2,1,0:T(8,128)(2,1)S(1)} %collective-permute-done.9.refs_5_) | copy-start | bytes 1572868
  44.4 3.8 %collective-permute-start.11 = (bf16[8,64,512]{2,1,0:T(8,128)(2,1)S(1)}, bf16[8,64,512]{2,1,0:T(8,128)(2,1)S(1)}, u32[]{:S(2)}, u32[]{:S(2)}) collective-permute-start(bf16[8,64,512]{2,1,0:T(8,128)(2,1)S(1)} %collective-permute-done.9.refs_5_), channel_id=1, source_target_pairs={{0,1},{1,0},{2,3},{3,2},{4,5},{5,4},{6,7},{7,6},{8,9},{9,8},{10,11... | collective-permute-start | bytes 1572872 | tf_op jit(solution)/shard_map/ppermute | solution.py:424
  44.7 3.5 %copy-start.4 = (bf16[8,64,512]{2,1,0:T(8,128)(2,1)}, bf16[8,64,512]{2,1,0:T(8,128)(2,1)S(1)}, u32[]{:S(2)}) copy-start(bf16[8,64,512]{2,1,0:T(8,128)(2,1)S(1)} %collective-permute-done.5.refs_1_) | copy-start | bytes 1572868
  44.7 3.4 %collective-permute-start.7 = (bf16[8,64,512]{2,1,0:T(8,128)(2,1)S(1)}, bf16[8,64,512]{2,1,0:T(8,128)(2,1)S(1)}, u32[]{:S(2)}, u32[]{:S(2)}) collective-permute-start(bf16[8,64,512]{2,1,0:T(8,128)(2,1)S(1)} %collective-permute-done.5.refs_1_), channel_id=1, source_target_pairs={{0,1},{1,0},{2,3},{3,2},{4,5},{5,4},{6,7},{7,6},{8,9},{9,8},{10,11... | collective-permute-start | bytes 1572872 | tf_op jit(solution)/shard_map/ppermute | solution.py:424
  45.8 2.5 %copy-start.10 = (bf16[512,512]{1,0:T(8,128)(2,1)S(1)}, bf16[512,512]{1,0:T(8,128)(2,1)}, u32[]{:S(2)}) copy-start(bf16[512,512]{1,0:T(8,128)(2,1)} %get-tuple-element.25.wvt_ref.wvt_hbm) | copy-start | bytes 1572868
  45.8 2.5 %copy-start.12 = (bf16[128,512]{1,0:T(8,128)(2,1)S(1)}, bf16[128,512]{1,0:T(8,128)(2,1)}, u32[]{:S(2)}) copy-start(bf16[128,512]{1,0:T(8,128)(2,1)} %cot_ref.1) | copy-start | bytes 393220
  45.8 2.5 %copy-start.13 = (bf16[4,128,256]{2,1,0:T(8,128)(2,1)S(1)}, bf16[4,128,256]{2,1,0:T(8,128)(2,1)}, u32[]{:S(2)}) copy-start(bf16[4,128,256]{2,1,0:T(8,128)(2,1)} %get-tuple-element.24.stack_ref.stack_hbm) | copy-start | bytes 786436
  45.9 12.4 %copy-start.16 = (bf16[8,64,512]{2,1,0:T(8,128)(2,1)}, bf16[8,64,512]{2,1,0:T(8,128)(2,1)S(1)}, u32[]{:S(2)}) copy-start(bf16[8,64,512]{2,1,0:T(8,128)(2,1)S(1)} %pad_maximum_fusion.1.refs_12_) | copy-start | bytes 1572868
  45.9 2.4 %copy-start.2 = (bf16[512,512]{1,0:T(8,128)(2,1)S(1)}, bf16[512,512]{1,0:T(8,128)(2,1)}, u32[]{:S(2)}) copy-start(bf16[512,512]{1,0:T(8,128)(2,1)} %wk_hbm.3) | copy-start | bytes 1572868
  45.9 2.4 %copy-start.9 = (s32[240,128,4]{1,2,0:T(4,128)S(1)}, s32[240,128,4]{1,2,0:T(4,128)}, u32[]{:S(2)}) copy-start(s32[240,128,4]{1,2,0:T(4,128)} %param.15) | copy-start | bytes 1474564
  46.0 12.0 %copy-start.17 = (bf16[8,64,512]{2,1,0:T(8,128)(2,1)}, bf16[8,64,512]{2,1,0:T(8,128)(2,1)S(1)}, u32[]{:S(2)}) copy-start(bf16[8,64,512]{2,1,0:T(8,128)(2,1)S(1)} %pad_maximum_fusion.refs_8_) | copy-start | bytes 1572868
  46.0 22.4 %collective-permute-start.18 = (bf16[8,64,512]{2,1,0:T(8,128)(2,1)S(1)}, bf16[8,64,512]{2,1,0:T(8,128)(2,1)S(1)}, u32[]{:S(2)}, u32[]{:S(2)}) collective-permute-start(bf16[8,64,512]{2,1,0:T(8,128)(2,1)S(1)} %pad_maximum_fusion.refs_8_), channel_id=1, source_target_pairs={{0,16},{1,17},{2,18},{3,19},{4,20},{5,21},{6,22},{7,23},{8,24},{9,... | collective-permute-start | bytes 1572872 | tf_op jit(solution)/shard_map/ppermute | solution.py:424
  46.8 4.4 %copy-start.5 = (bf16[8,64,512]{2,1,0:T(8,128)(2,1)}, bf16[8,64,512]{2,1,0:T(8,128)(2,1)S(1)}, u32[]{:S(2)}) copy-start(bf16[8,64,512]{2,1,0:T(8,128)(2,1)S(1)} %collective-permute-done.10.refs_6_) | copy-start | bytes 1572868
  46.8 16.3 %collective-permute-start.21 = (bf16[8,64,512]{2,1,0:T(8,128)(2,1)S(1)}, bf16[8,64,512]{2,1,0:T(8,128)(2,1)S(1)}, u32[]{:S(2)}, u32[]{:S(2)}) collective-permute-start(bf16[8,64,512]{2,1,0:T(8,128)(2,1)S(1)} %pad_maximum_fusion.1.refs_12_), channel_id=1, source_target_pairs={{0,8},{1,9},{2,10},{3,11},{4,12},{5,13},{6,14},{7,15},{8,0},{9,1},... | collective-permute-start | bytes 1572872 | tf_op jit(solution)/shard_map/ppermute | solution.py:424
  48.2 3.1 %copy-start.6 = (bf16[8,64,512]{2,1,0:T(8,128)(2,1)}, bf16[8,64,512]{2,1,0:T(8,128)(2,1)S(1)}, u32[]{:S(2)}) copy-start(bf16[8,64,512]{2,1,0:T(8,128)(2,1)S(1)} %collective-permute-done.6.refs_2_) | copy-start | bytes 1572868
  48.2 3.1 %copy-start.7 = (bf16[8,64,512]{2,1,0:T(8,128)(2,1)}, bf16[8,64,512]{2,1,0:T(8,128)(2,1)S(1)}, u32[]{:S(2)}) copy-start(bf16[8,64,512]{2,1,0:T(8,128)(2,1)S(1)} %collective-permute-done.11.refs_7_) | copy-start | bytes 1572868
  48.2 3.1 %copy-start.8 = (bf16[8,64,512]{2,1,0:T(8,128)(2,1)}, bf16[8,64,512]{2,1,0:T(8,128)(2,1)S(1)}, u32[]{:S(2)}) copy-start(bf16[8,64,512]{2,1,0:T(8,128)(2,1)S(1)} %collective-permute-done.7.refs_3_) | copy-start | bytes 1572868
  51.3 17.1 %all-to-all-start = ((f32[32,16,128]{2,1,0:T(8,128)}), f32[32,16,128]{2,1,0:T(8,128)S(1)}, u32[]{:S(2)}, u32[]{:S(2)}) async-start(f32[32,16,128]{2,1,0:T(8,128)} %get-tuple-element.37.stats_hbm), calls=%async_computation | async-start | bytes 524288 | tf_op jit(solution)/shard_map/all_to_all | solution.py:558
  58.0 11.0 %collective-permute-start.19 = (bf16[8,64,512]{2,1,0:T(8,128)(2,1)S(1)}, bf16[8,64,512]{2,1,0:T(8,128)(2,1)S(1)}, u32[]{:S(2)}, u32[]{:S(2)}) collective-permute-start(bf16[8,64,512]{2,1,0:T(8,128)(2,1)S(1)} %pad_maximum_fusion.refs_8_), channel_id=1, source_target_pairs={{0,1},{1,0},{2,3},{3,2},{4,5},{5,4},{6,7},{7,6},{8,9},{9,8},{10,11... | collective-permute-start | bytes 1572872 | tf_op jit(solution)/shard_map/ppermute | solution.py:424
  58.3 10.6 %collective-permute-start.22 = (bf16[8,64,512]{2,1,0:T(8,128)(2,1)S(1)}, bf16[8,64,512]{2,1,0:T(8,128)(2,1)}, u32[]{:S(2)}, u32[]{:S(2)}) collective-permute-start(bf16[8,64,512]{2,1,0:T(8,128)(2,1)S(1)} %pad_maximum_fusion.1.refs_12_), channel_id=1, source_target_pairs={{0,1},{1,0},{2,3},{3,2},{4,5},{5,4},{6,7},{7,6},{8,9},{9,8},{10,11... | collective-permute-start | bytes 1572872 | tf_op jit(solution)/shard_map/ppermute | solution.py:424
  63.1 8.0 %copy-start.21 = (bf16[8,64,512]{2,1,0:T(8,128)(2,1)}, bf16[8,64,512]{2,1,0:T(8,128)(2,1)S(1)}, u32[]{:S(2)}) copy-start(bf16[8,64,512]{2,1,0:T(8,128)(2,1)S(1)} %collective-permute-done.21.refs_13_) | copy-start | bytes 1572868
  68.4 2.7 %copy-start.18 = (f32[32,16,128]{2,1,0:T(8,128)}, f32[32,16,128]{2,1,0:T(8,128)S(1)}, u32[]{:S(2)}) copy-start(f32[32,16,128]{2,1,0:T(8,128)S(1)} %all-to-all-done.stats_all_ref) | copy-start | bytes 786436
  68.4 2.7 %copy-start.20 = (bf16[8,64,512]{2,1,0:T(8,128)(2,1)}, bf16[8,64,512]{2,1,0:T(8,128)(2,1)S(1)}, u32[]{:S(2)}) copy-start(bf16[8,64,512]{2,1,0:T(8,128)(2,1)S(1)} %collective-permute-done.18.refs_9_) | copy-start | bytes 1572868
  68.4 2.0 %collective-permute-start.20 = (bf16[8,64,512]{2,1,0:T(8,128)(2,1)S(1)}, bf16[8,64,512]{2,1,0:T(8,128)(2,1)S(1)}, u32[]{:S(2)}, u32[]{:S(2)}) collective-permute-start(bf16[8,64,512]{2,1,0:T(8,128)(2,1)S(1)} %collective-permute-done.18.refs_9_), channel_id=1, source_target_pairs={{0,1},{1,0},{2,3},{3,2},{4,5},{5,4},{6,7},{7,6},{8,9},{9,8},{10,11... | collective-permute-start | bytes 1572872 | tf_op jit(solution)/shard_map/ppermute | solution.py:424
  68.8 2.3 %collective-permute-start.23 = (bf16[8,64,512]{2,1,0:T(8,128)(2,1)S(1)}, bf16[8,64,512]{2,1,0:T(8,128)(2,1)S(1)}, u32[]{:S(2)}, u32[]{:S(2)}) collective-permute-start(bf16[8,64,512]{2,1,0:T(8,128)(2,1)S(1)} %collective-permute-done.21.refs_13_), channel_id=1, source_target_pairs={{0,1},{1,0},{2,3},{3,2},{4,5},{5,4},{6,7},{7,6},{8,9},{9,8},{10,11... | collective-permute-start | bytes 1572872 | tf_op jit(solution)/shard_map/ppermute | solution.py:424
  68.9 2.2 %copy-start.22 = (bf16[8,64,512]{2,1,0:T(8,128)(2,1)}, bf16[8,64,512]{2,1,0:T(8,128)(2,1)S(1)}, u32[]{:S(2)}) copy-start(bf16[8,64,512]{2,1,0:T(8,128)(2,1)S(1)} %collective-permute-done.19.refs_10_) | copy-start | bytes 1572868
  70.4 0.8 %copy-start.23 = (bf16[8,64,512]{2,1,0:T(8,128)(2,1)}, bf16[8,64,512]{2,1,0:T(8,128)(2,1)S(1)}, u32[]{:S(2)}) copy-start(bf16[8,64,512]{2,1,0:T(8,128)(2,1)S(1)} %collective-permute-done.20.refs_11_) | copy-start | bytes 1572868
  71.1 0.8 %copy-start.24 = (bf16[8,64,512]{2,1,0:T(8,128)(2,1)}, bf16[8,64,512]{2,1,0:T(8,128)(2,1)S(1)}, u32[]{:S(2)}) copy-start(bf16[8,64,512]{2,1,0:T(8,128)(2,1)S(1)} %collective-permute-done.23.refs_15_) | copy-start | bytes 1572868
where the time goes:
time: 77.4 us; the launch traced here: 77.5 us
  starting transfers between devices  28.6 us (37%)
  waiting for transfers between devices  21.9 us (28%)
  Pallas kernels  21.1 us (27%)
  local copies, waits for them, and re-layouts  3.87 us (5%)
  between operations  1.8 us (2%)
    ppermute x24, starting transfers between devices, swap(): return lax.ppermute(block, axes, [(i, i ^ mask) for i in range(count)])  21.9 us
    ppermute x24, waiting for transfers between devices, swap(): return lax.ppermute(block, axes, [(i, i ^ mask) for i in range(count)])  16.7 us
    all_to_all x1, starting transfers between devices, local(): stats_all = lax.all_to_all(stats, axes, 0, 0, tiled=True)  6.68 us
    pallas_call x1, Pallas kernels, local(): pl.pallas_call(functools.partial(key_grad_kernel, sizes, bits), out_shape...  5.59 us
    all_to_all x1, waiting for transfers between devices, local(): stats_all = lax.all_to_all(stats, axes, 0, 0, tiled=True)  5.21 us
    pallas_call x1, Pallas kernels, local(): pl.pallas_call(functools.partial(query_grad_kernel, sizes), out_shape=sha...  4.55 us
    pallas_call x1, Pallas kernels, local(): pl.pallas_call(prepare_kernel, out_shape=(stacks, stacks, own, own, squar...  3.35 us
    pallas_call x2, Pallas kernels, work(): pl.pallas_call(functools.partial(kernel, sizes), out_shape=shape((2 * cou...  3.01 us
  transfers between devices with their start and end apart: 25, of which 10 were waited for; matrix products, arithmetic and copies ran while one was open for 2% of the time, Pallas kernels for 18%

commit v1 on v0

--- a/solution.py
+++ b/solution.py
@@ -51,14 +51,11 @@
         reader, blk = far // self.blks, lax.rem(far, self.blks)
         return reader, blk // 2, blk & 1
 
-    def row_place(self, order, device):
+    def row_place(self, device):
         reader, line, core = self.apart(device)
-        for at, bit in enumerate(order[:-1]):
-            line = line + (jnp.right_shift(reader, bit) & 1) * ((self.blks // 2) << at)
-        return (jnp.right_shift(reader, order[-1]) & 1) + 2 * core, line
-
-    def orders(self):
-        return orders(self.readers)
+        near = line == 0
+        group = jnp.where(near, core, 2 + reader + self.readers * core)
+        return group, jnp.where(near, reader, line - 1)
 
     def half_place(self, bit, device):
         reader, line, core = self.apart(device)
@@ -68,11 +65,6 @@
         low = reader & ((1 << bit) - 1)
         rest = low + (jnp.right_shift(reader, bit + 1) << bit)
         return rest + self.readers // 2 * core, 2 * line + first
-
-
-def orders(readers):
-    rising = tuple(range((readers - 1).bit_length()))
-    return rising, rising[::-1]
 
 
 def start_copy(place, refs, make):
@@ -209,27 +201,24 @@
 
 class Rows:
     def __init__(self, layout, groups, mask_ref, buf, words, sems, block):
-        self.layout, self.halves, self.mask_ref = layout, (groups[:4], groups[4:]), mask_ref
+        self.layout, self.groups, self.mask_ref = layout, groups, mask_ref
         self.buf, self.words, self.sems, self.block = buf, words, sems, block
 
-    def rows(self, slot, t, k):
-        half = self.block // 2
-        into = self.buf.at[slot, pl.ds(t * self.block + k * half, half)]
-        return lambda src: pltpu.make_async_copy(src.at[pl.ds(0, half)], into, self.sems.at[slot, t, k])
+    def rows(self, slot, t):
+        into = self.buf.at[slot, pl.ds(t * self.block, self.block)]
+        return lambda src: pltpu.make_async_copy(src, into, self.sems.at[slot, t, 0])
 
     def mask(self, slot, t, pattern):
-        return pltpu.make_async_copy(self.mask_ref.at[pattern], self.words.at[slot, t], self.sems.at[slot, t, 2])
+        return pltpu.make_async_copy(self.mask_ref.at[pattern], self.words.at[slot, t], self.sems.at[slot, t, 1])
 
     def start(self, slot, blocks, patterns):
         for t in range(TILES):
-            for k, order in enumerate(self.layout.orders()):
-                start_copy(self.layout.row_place(order, blocks[t]), self.halves[k], self.rows(slot, t, k))
+            start_copy(self.layout.row_place(blocks[t]), self.groups, self.rows(slot, t))
             self.mask(slot, t, jnp.maximum(patterns[t], 0)).start()
 
     def wait(self, slot):
         for t in range(TILES):
-            for k in range(2):
-                self.rows(slot, t, k)(self.halves[k][0].at[0]).wait()
+            self.rows(slot, t)(self.groups[0].at[0]).wait()
             self.mask(slot, t, 0).wait()
 
     def bias(self, slot, blocks, patterns):
@@ -240,7 +229,8 @@
 
 
 def forward_kernel(sizes, work_ref, stack_ref, cot_ref, wk_ref, wvt_ref, mask_ref, *refs):
-    groups, refs = refs[:8], refs[8:]
+    count = 2 + 2 * sizes[0]
+    groups, refs = refs[:count], refs[count:]
     out_ref, sent_ref, stats_ref, buf, words, bias_ref, max_ref, sum_ref, acc_ref, score_ref, sems = refs
     layout = Layout(*sizes)
     block, width = cot_ref.shape
@@ -292,7 +282,8 @@
 def query_grad_kernel(
     sizes, work_ref, stack_hbm, cot_stack_hbm, stats_hbm, wqt_hbm, wk_hbm, wkt_hbm, wv_hbm, mask_ref, *refs
 ):
-    groups, refs = refs[:8], refs[8:]
+    count = 2 + 2 * sizes[0]
+    groups, refs = refs[:count], refs[count:]
     part_ref, stack_ref, cot_stack_ref, stats_ref, wqt_ref, wk_ref, wkt_ref, wv_ref = refs[:8]
     buf, words, bias_ref, acc_ref, score_ref, d_prob_ref, sems, w_sems = refs[8:]
     layout = Layout(*sizes)
@@ -339,7 +330,8 @@
     sizes, bits, work_ref, key_hbm, value_hbm, wq_hbm, wkt_hbm, wvt_hbm, part_hbm, mask_ref, stats_all_ref, *refs
 ):
     readers = sizes[0]
-    groups, refs = refs[:8], refs[8:]
+    count = 2 + 2 * readers
+    groups, refs = refs[:count], refs[count:]
     halves, refs = (refs[:readers], refs[readers : 2 * readers]), refs[2 * readers :]
     out_ref, key_ref, value_ref, part_ref, wq_ref, wkt_ref, wvt_ref, buf, words, cot_buf, stats, bias_ref = refs[:12]
     query_stack_ref, cot_stack_ref, score_ref, d_prob_ref, key_acc, value_acc, sems, c_sems, w_sems = refs[12:]
@@ -428,12 +420,6 @@
     return lax.optimization_barrier((value, *others))[0]
 
 
-def over_readers(chunk, order, blks):
-    for bit in order[:-1]:
-        chunk = jnp.concatenate([chunk, swap(chunk, blks << bit)], 0)
-    return [chunk, swap(chunk, blks << order[-1])]
-
-
 def local(features, cotangent, w_query, w_key, w_value, tile_coords, tile_count, mask_table):
     block, width = features.shape
     readers, blks, cap = lax.axis_size("reader"), lax.axis_size("blk"), tile_coords.shape[2]
@@ -466,19 +452,21 @@
     )(features, tile_coords.transpose(0, 3, 1, 2), tile_count)
     lined = [packed] + [swap(packed, 2 * k) for k in range(1, lines)]
 
+    nearest_first = sorted(range(1, readers), key=lambda k: (k.bit_count(), k))
+
+    def to_readers(block):
+        there = {k: swap(block, blks * k) for k in nearest_first}
+        return [there[k] for k in range(1, readers)]
+
+    columns = [packed] + to_readers(packed)
+
     bits = (0, (readers - 1).bit_length() - 1)
-    cot_parts = [
-        jnp.concatenate([cotangent[None, half * k : half * (k + 1)], packed[:, block:]], 1) for k in range(2)
-    ]
+    cot_parts = [cotangent[None, half * k : half * (k + 1)] for k in range(2)]
     cot_other = [swap(part, blks << bit) for part, bit in zip(cot_parts, bits)]
 
-    own_list = packed[:, block:, :128]
-    columns = {1 << bit: other[:, half:, :128] for bit, other in zip(bits, cot_other)}
+    column_lists = jnp.concatenate([entry[:, block:, :128] for entry in columns], 0)
     line_lists = jnp.concatenate([entry[:, block:, :128] for entry in lined], 0)
     row_lists = jnp.concatenate([line_lists, swap(line_lists, 1)], 0)
-    far_list = after(own_list, row_lists)
-    columns = {k: columns[k] if k in columns else swap(far_list, blks * k) for k in range(1, readers)}
-    column_lists = jnp.concatenate([own_list] + [columns[k] for k in range(1, readers)], 0)
 
     def work(kernel, lists, count, name):
         return pl.pallas_call(
@@ -509,21 +497,23 @@
         compiler_params=most,
         cost_estimate=cost(2),
         name="prepare",
-    )(features, cotangent, w_query, w_key, w_value)
+    )(after(features, row_lists), cotangent, w_query, w_key, w_value)
     query_stack, cot_stack, keys, values, w_query_t, w_key_t, w_value_t = prepared
 
-    lined = after(lined, prepared)
-    chunks = [jnp.concatenate([entry[:, half * k : half * (k + 1)] for entry in lined], 0) for k in range(2)]
-    here = [over_readers(chunk, order, blks) for chunk, order in zip(chunks, orders(readers))]
-    rows_all = []
-    for first, last in here:
-        rows_all += [first, last, swap(first, 1), swap(last, 1)]
-
-    pairs = [part[:, :half] for k in range(2) for part in (cot_parts[k], cot_other[k])]
-    pieces = [after(jnp.concatenate(pairs, 0), *chunks, row_lists)]
+    near = jnp.concatenate([entry[:, :block] for entry in columns], 0)
+    line = jnp.concatenate([entry[:, :block] for entry in lined[1:]], 0)
+    line = after(line, columns, cot_other)
+    here = [line] + to_readers(line)
+    other_near = swap(after(near, query_work), 1)
+    other_line = swap(after(line, query_work), 1)
+    rows_all = [near, other_near, *here, other_line] + [swap(group, 1) for group in here[1:]]
+
+    pairs = [part for k in range(2) for part in (cot_parts[k], cot_other[k])]
+    pieces = [after(jnp.concatenate(pairs, 0), line, row_lists)]
+    done_first = (query_work, key_work, prepared)
     mask = blks // 2
     while mask > 1:
-        pieces += [swap(after(piece, query_work, key_work) if at else piece, mask) for at, piece in enumerate(pieces)]
+        pieces += [swap(after(piece, done_first) if at else piece, mask) for at, piece in enumerate(pieces)]
         mask //= 2
 
     cots_here = []
@@ -542,12 +532,12 @@
     met = pltpu.VMEM((HEADS, TILES * block, block), f32)
     pair_met = pltpu.VMEM((HEADS // 2, block, 2 * TILES * block), f32)
     pair_rows = pltpu.VMEM((HEADS // 2, 2 * TILES * block, 2 * head), bf16)
-    row_sems = pltpu.SemaphoreType.DMA((2, TILES, 3))
+    row_sems = pltpu.SemaphoreType.DMA((2, TILES, 2))
 
     attn_out, stats = pl.pallas_call(
         functools.partial(forward_kernel, sizes),
         out_shape=(own, shape((devices, 2 * HEADS, block), f32)),
-        in_specs=[SMEM] + [VMEM] * 4 + [HBM] * 9,
+        in_specs=[SMEM] + [VMEM] * 4 + [HBM] * (3 + 2 * readers),
         out_specs=(VMEM, VMEM),
         scratch_shapes=[own_stats, buffer, word_buffer, bias, per_head, per_head, turned, met, row_sems],
         compiler_params=some,
@@ -560,7 +550,7 @@
     query_part = pl.pallas_call(
         functools.partial(query_grad_kernel, sizes),
         out_shape=shape((block, width), f32),
-        in_specs=[SMEM] + [HBM] * 16,
+        in_specs=[SMEM] + [HBM] * (10 + 2 * readers),
         out_specs=VMEM,
         scratch_shapes=[
             stack_space, stack_space, own_stats, weight, weight, weight, weight, buffer, word_buffer, bias, turned,
@@ -574,12 +564,12 @@
     cots_all = []
     for first, rest in cots_here:
         cots_all += [first, *rest, swap(after(first, stats), 1)]
-        cots_all += [swap(after(part, stats_all, query_part), 1) for part in rest]
+        cots_all += [swap(after(part, query_part), 1) for part in rest]
 
     grad_features = pl.pallas_call(
         functools.partial(key_grad_kernel, sizes, bits),
         out_shape=own,
-        in_specs=[SMEM] + [HBM] * (16 + 2 * readers),
+        in_specs=[SMEM] + [HBM] * (10 + 4 * readers),
         out_specs=VMEM,
         scratch_shapes=[
             rows_low, rows_low, rows_wide, weight, weight, weight,

time: 77.4 us -> 94.6 us (1.22)
  blocking collectives: 0 us -> 16.4 us
  waiting for transfers between devices: 21.9 us -> 16.1 us
  Pallas kernels: 21.1 us -> 23.2 us
  starting transfers between devices: 28.6 us -> 30.7 us
  other arithmetic: 0.28 us -> 1.89 us
    all_to_all x0 -> x1, blocking collectives: none -> 16.4 us  [local(): stats_all = lax.all_to_all(stats, axes, 0, 0, tiled=True)]
    ppermute x24 -> x26, starting transfers between devices: 21.9 us -> 30.7 us  [swap(): return lax.ppermute(block, axes, [(i, i ^ mask) for i in range(count)])]
    all_to_all x1 -> x0, starting transfers between devices: 6.68 us -> none  [local(): stats_all = lax.all_to_all(stats, axes, 0, 0, tiled=True)]
    all_to_all x1 -> x0, waiting for transfers between devices: 5.21 us -> none  [local(): stats_all = lax.all_to_all(stats, axes, 0, 0, tiled=True)]
    concatenate x2, other arithmetic: 0.14 us -> 1.71 us  [local(): part = jnp.concatenate([piece[2 * k:2 * k + 2] for piece in pieces], 0)]
    pallas_call x1, Pallas kernels: 2.94 us -> 4.22 us  [local(): pl.pallas_call(functools.partial(forward_kernel, sizes), out_shape=(own,...]
    unnamed x52 -> x58, local copies, waits for them, and re-layouts: 2.05 us -> 3.33 us
    pallas_call x1, Pallas kernels: 4.55 us -> 5.54 us  [local(): pl.pallas_call(functools.partial(query_grad_kernel, sizes), out_shape=sha...]
  transfers between devices with their start and end apart: 25 -> 26, of which waited for: 10 -> 6; matrix products, arithmetic and copies ran while one was open for 2% -> 2% of each run, Pallas kernels for 18% -> 17%
where the time goes in v1:
time: 94.6 us; the launch traced here: 94.5 us
  starting transfers between devices  30.7 us (32%)
  Pallas kernels  23.2 us (25%)
  blocking collectives  16.4 us (17%)
  waiting for transfers between devices  16.1 us (17%)
  local copies, waits for them, and re-layouts  4.38 us (5%)
  other arithmetic  1.89 us (2%)
  between operations  1.86 us (2%)
    ppermute x26, starting transfers between devices, swap(): return lax.ppermute(block, axes, [(i, i ^ mask) for i in range(count)])  30.7 us
    all_to_all x1, blocking collectives, local(): stats_all = lax.all_to_all(stats, axes, 0, 0, tiled=True)  16.4 us
    ppermute x26, waiting for transfers between devices, swap(): return lax.ppermute(block, axes, [(i, i ^ mask) for i in range(count)])  16.1 us
    pallas_call x1, Pallas kernels, local(): pl.pallas_call(functools.partial(key_grad_kernel, sizes, bits), out_shape...  5.56 us
    pallas_call x1, Pallas kernels, local(): pl.pallas_call(functools.partial(query_grad_kernel, sizes), out_shape=sha...  5.54 us
    pallas_call x1, Pallas kernels, local(): pl.pallas_call(functools.partial(forward_kernel, sizes), out_shape=(own,...  4.22 us
    unnamed x58, local copies, waits for them, and re-layouts  3.33 us
    pallas_call x1, Pallas kernels, local(): pl.pallas_call(prepare_kernel, out_shape=(stacks, stacks, own, own, squar...  3.31 us
  transfers between devices with their start and end apart: 26, of which 6 were waited for; matrix products, arithmetic and copies ran while one was open for 2% of the time, Pallas kernels for 17%

profile of v1, /device:TPU:0, one launch (start us, length us, event | category | flops | bytes accessed | tf_op | source)
XLA Modules:
  0.0 94.5 jit_solution(4669911516442740844)
XLA Ops:
  1.3 0.0 copy-start.13
  1.3 1.6 %pack.1 = bf16[1,144,512]{2,1,0:T(8,128)(2,1)} custom-call(bf16[128,512]{1,0:T(8,128)(2,1)} %own_hbm.2, s32[1,3,1,8]{3,2,1,0:T(1,128)} %bitcast.13, s32[1,1]{1,0:T(1,128)S(6)} %copy.14.count_hbm), custom_call_target="tpu_custom_call" | custom-call | tf_op jit(solution)/shard_map/pack/pallas_call | solution.py:442
  2.9 5.1 %collective-permute-start.2 = (bf16[1,144,512]{2,1,0:T(8,128)(2,1)}, bf16[1,144,512]{2,1,0:T(8,128)(2,1)S(1)}, u32[]{:S(2)}, u32[]{:S(2)}) collective-permute-start(bf16[1,144,512]{2,1,0:T(8,128)(2,1)} %pack.1), channel_id=1, source_target_pairs={{0,6},{1,7},{2,4},{3,5},{4,2},{5,3},{6,0},{7,1},{8,14},{9,15},{10,... | collective-permute-start | bytes 442376 | tf_op jit(solution)/shard_map/ppermute | solution.py:416
  8.0 0.6 collective-permute-start
  8.7 1.7 %collective-permute-start.9 = (bf16[1,64,512]{2,1,0:T(8,128)(2,1)S(1)}, bf16[1,64,512]{2,1,0:T(8,128)(2,1)S(1)}, u32[]{:S(2)}, u32[]{:S(2)}) collective-permute-start(bf16[1,64,512]{2,1,0:T(8,128)(2,1)S(1)} %get-tuple-element.60), channel_id=1, source_target_pairs={{0,16},{1,17},{2,18},{3,19},{4,20},{5,21},{6,22},{7,23},{8,24},{9,... | collective-permute-start | bytes 196616 | tf_op jit(solution)/shard_map/ppermute | solution.py:416
  10.4 1.5 %collective-permute-start.8 = (bf16[1,64,512]{2,1,0:T(8,128)(2,1)S(1)}, bf16[1,64,512]{2,1,0:T(8,128)(2,1)S(1)}, u32[]{:S(2)}, u32[]{:S(2)}) collective-permute-start(bf16[1,64,512]{2,1,0:T(8,128)(2,1)S(1)} %get-tuple-element.61), channel_id=1, source_target_pairs={{0,8},{1,9},{2,10},{3,11},{4,12},{5,13},{6,14},{7,15},{8,0},{9,1},... | collective-permute-start | bytes 196616 | tf_op jit(solution)/shard_map/ppermute | solution.py:416
  11.9 1.1 %collective-permute-done.9 = bf16[1,64,512]{2,1,0:T(8,128)(2,1)S(1)} collective-permute-done((bf16[1,64,512]{2,1,0:T(8,128)(2,1)S(1)}, bf16[1,64,512]{2,1,0:T(8,128)(2,1)S(1)}, u32[]{:S(2)}, u32[]{:S(2)}) %collective-permute-start.9) | collective-permute-done | bytes 65568 | tf_op jit(solution)/shard_map/ppermute | solution.py:416
  13.0 2.6 %collective-permute-start.6 = (bf16[1,144,512]{2,1,0:T(8,128)(2,1)S(1)}, bf16[1,144,512]{2,1,0:T(8,128)(2,1)S(1)}, u32[]{:S(2)}, u32[]{:S(2)}) collective-permute-start(bf16[1,144,512]{2,1,0:T(8,128)(2,1)S(1)} %copy-done.20), channel_id=1, source_target_pairs={{0,24},{1,25},{2,26},{3,27},{4,28},{5,29},{6,30},{7,31},{8,16},{9,... | collective-permute-start | bytes 442376 | tf_op jit(solution)/shard_map/ppermute | solution.py:416
  15.6 0.5 collective-permute-start.5
  16.1 0.6 collective-permute-start.4
  16.7 0.1 copy-done.27
  16.8 3.9 %collective-permute-done.1 = bf16[1,144,512]{2,1,0:T(8,128)(2,1)S(1)} collective-permute-done((bf16[1,144,512]{2,1,0:T(8,128)(2,1)}, bf16[1,144,512]{2,1,0:T(8,128)(2,1)S(1)}, u32[]{:S(2)}, u32[]{:S(2)}) %collective-permute-start.1) | collective-permute-done | bytes 147488 | tf_op jit(solution)/shard_map/ppermute | solution.py:416
  20.7 0.0 slice-start
  20.8 0.9 slice-done
  21.7 0.0 collective-permute-done.6
  21.7 0.0 collective-permute-done.4
  21.7 2.5 %collective-permute-start.12 = (bf16[3,128,512]{2,1,0:T(8,128)(2,1)S(1)}, bf16[3,128,512]{2,1,0:T(8,128)(2,1)S(1)}, u32[]{:S(2)}, u32[]{:S(2)}) collective-permute-start(bf16[3,128,512]{2,1,0:T(8,128)(2,1)S(1)} %pad_maximum_fusion.3.refs_2_), channel_id=1, source_target_pairs={{0,24},{1,25},{2,26},{3,27},{4,28},{5,29},{6,30},{7,31},{8,16},{9,... | collective-permute-start | bytes 1179656 | tf_op jit(solution)/shard_map/ppermute | solution.py:416
  24.2 0.5 collective-permute-start.11
  24.8 0.5 collective-permute-start.10
  25.3 0.1 collective-permute-start.3
  25.5 0.1 pad_maximum_fusion.refs_0_
  25.6 1.3 %key_work.1.work_ref = s32[69]{0:T(128)S(1)} custom-call(s32[4,128]{1,0:T(4,128)S(1)} %bitcast.12), custom_call_target="tpu_custom_call" | custom-call | flops 200000000 | bytes 4000000 | tf_op jit(solution)/shard_map/key_work/pallas_call | solution.py:472
  26.9 0.0 collective-permute-done.3
  26.9 0.5 copy-done.19
  27.5 2.5 %collective-permute-start.18 = (bf16[4,64,512]{2,1,0:T(8,128)(2,1)S(1)}, bf16[4,64,512]{2,1,0:T(8,128)(2,1)S(1)}, u32[]{:S(2)}, u32[]{:S(2)}) collective-permute-start(bf16[4,64,512]{2,1,0:T(8,128)(2,1)S(1)} %pad_maximum_fusion.4), channel_id=1, source_target_pairs={{0,2},{1,3},{2,0},{3,1},{4,6},{5,7},{6,4},{7,5},{8,10},{9,11},{10,... | collective-permute-start | bytes 786440 | tf_op jit(solution)/shard_map/ppermute | solution.py:416
  30.1 2.2 %collective-permute-start.17 = (bf16[4,64,512]{2,1,0:T(8,128)(2,1)S(1)}, bf16[4,64,512]{2,1,0:T(8,128)(2,1)S(1)}, u32[]{:S(2)}, u32[]{:S(2)}) collective-permute-start(bf16[4,64,512]{2,1,0:T(8,128)(2,1)S(1)} %pad_maximum_fusion.4), channel_id=1, source_target_pairs={{0,4},{1,5},{2,6},{3,7},{4,0},{5,1},{6,2},{7,3},{8,12},{9,13},{10,... | collective-permute-start | bytes 786440 | tf_op jit(solution)/shard_map/ppermute | solution.py:416
  32.3 1.6 %query_work.1.work_ref = s32[133]{0:T(256)S(1)} custom-call(s32[8,128]{1,0:T(8,128)S(1)} %bitcast.11), custom_call_target="tpu_custom_call" | custom-call | flops 200000000 | bytes 4000000 | tf_op jit(solution)/shard_map/query_work/pallas_call | solution.py:472
  33.9 0.0 copy-start.18
  33.9 3.3 %prepare.1 = (bf16[4,128,256]{2,1,0:T(8,128)(2,1)}, bf16[4,128,256]{2,1,0:T(8,128)(2,1)}, bf16[128,512]{1,0:T(8,128)(2,1)}, bf16[128,512]{1,0:T(8,128)(2,1)}, bf...) custom-call(bf16[128,512]{1,0:T(8,128)(2,1)} %own_hbm.2, bf16[128,512]{1,0:T(8,128)(2,1)} %cot_ref.1, ...), custom_call_target="tpu_custom_call" | custom-call | flops 400000000 | bytes 4000000 | tf_op jit(solution)/shard_map/prepare/pallas_call | solution.py:491
  37.2 4.6 %collective-permute-done.17 = bf16[4,64,512]{2,1,0:T(8,128)(2,1)S(1)} collective-permute-done((bf16[4,64,512]{2,1,0:T(8,128)(2,1)S(1)}, bf16[4,64,512]{2,1,0:T(8,128)(2,1)S(1)}, u32[]{:S(2)}, u32[]{:S(2)}) %collective-permute-start.17) | collective-permute-done | bytes 262176 | tf_op jit(solution)/shard_map/ppermute | solution.py:416
  41.9 4.6 %collective-permute-start.19 = (bf16[4,64,512]{2,1,0:T(8,128)(2,1)S(1)}, bf16[4,64,512]{2,1,0:T(8,128)(2,1)S(1)}, u32[]{:S(2)}, u32[]{:S(2)}) collective-permute-start(bf16[4,64,512]{2,1,0:T(8,128)(2,1)S(1)} %collective-permute-done.17), channel_id=1, source_target_pairs={{0,2},{1,3},{2,0},{3,1},{4,6},{5,7},{6,4},{7,5},{8,10},{9,11},{10,... | collective-permute-start | bytes 786440 | tf_op jit(solution)/shard_map/ppermute | solution.py:416
  46.5 0.0 collective-permute-done.18
  46.5 0.1 collective-permute-start.7
  46.6 0.0 collective-permute-done.12.refs_5_
  46.6 0.6 collective-permute-start.13
  47.2 0.0 collective-permute-done.11.refs_4_
  47.2 0.1 collective-permute-start.16
  47.3 0.0 collective-permute-done.10.refs_3_
  47.3 0.4 collective-permute-start.15
  47.7 4.9 %collective-permute-done.19 = bf16[4,64,512]{2,1,0:T(8,128)(2,1)S(1)} collective-permute-done((bf16[4,64,512]{2,1,0:T(8,128)(2,1)S(1)}, bf16[4,64,512]{2,1,0:T(8,128)(2,1)S(1)}, u32[]{:S(2)}, u32[]{:S(2)}) %collective-permute-start.19) | collective-permute-done | bytes 262176 | tf_op jit(solution)/shard_map/ppermute | solution.py:416
  52.6 0.0 copy-start.14
  52.6 0.9 pad_maximum_fusion.2.refs_14_
  53.5 0.9 pad_maximum_fusion.1.refs_10_
  54.3 1.9 %collective-permute-start.20 = (bf16[8,64,512]{2,1,0:T(8,128)(2,1)}, bf16[8,64,512]{2,1,0:T(8,128)(2,1)S(1)}, u32[]{:S(2)}, u32[]{:S(2)}) collective-permute-start(bf16[8,64,512]{2,1,0:T(8,128)(2,1)} %pad_maximum_fusion.1.refs_10_), channel_id=1, source_target_pairs={{0,16},{1,17},{2,18},{3,19},{4,20},{5,21},{6,22},{7,23},{8,24},{9,... | collective-permute-start | bytes 1572872 | tf_op jit(solution)/shard_map/ppermute | solution.py:416
  56.3 1.6 %collective-permute-start.23 = (bf16[8,64,512]{2,1,0:T(8,128)(2,1)}, bf16[8,64,512]{2,1,0:T(8,128)(2,1)S(1)}, u32[]{:S(2)}, u32[]{:S(2)}) collective-permute-start(bf16[8,64,512]{2,1,0:T(8,128)(2,1)} %pad_maximum_fusion.2.refs_14_), channel_id=1, source_target_pairs={{0,8},{1,9},{2,10},{3,11},{4,12},{5,13},{6,14},{7,15},{8,0},{9,1},... | collective-permute-start | bytes 1572872 | tf_op jit(solution)/shard_map/ppermute | solution.py:416
  57.8 0.0 collective-permute-done.16.refs_9_
  57.8 0.0 collective-permute-done.15.refs_8_
  58.0 4.2 %forward.1 = (bf16[128,512]{1,0:T(8,128)(2,1)}, f32[32,16,128]{2,1,0:T(8,128)S(1)}) custom-call(s32[133]{0:T(256)S(1)} %query_work.1.work_ref, bf16[4,128,256]{2,1,0:T(8,128)(2,1)S(1)} %copy-done.15, bf16[128,512]{1,0:T(8,128)(2,1)S(1)} %copy-done.14, bf16[512,512]{1,0:T(8,128)(2,1)S(1)} %copy-done.2, bf16[512,512]{1,0:T(8,128)(2,1)S(1)} %copy-done.12, ...), custom_call_target="tpu_custom_call" | custom-call | flops 1000000000 | bytes 4000000 | tf_op jit(solution)/shard_map/forward/pallas_call | solution.py:537
  62.3 0.7 copy-done.16
  63.0 0.5 collective-permute-start.24
  63.5 5.5 %query_grad.1.part_hbm = f32[128,512]{1,0:T(8,128)} custom-call(s32[133]{0:T(256)} %copy-done.18, bf16[4,128,256]{2,1,0:T(8,128)(2,1)} %get-tuple-element.24.stack_ref.stack_hbm, bf16[4,128,256]{2,1,0:T(8,128)(2,1)} %get-tuple-element.33.cot_stack_hbm, f32[32,16,128]{2,1,0:T(8,128)} %copy-done.16, bf16[512,512]{1,0:T(8,128)(2,1)} %get-tuple-element.35.wqt_hbm, ...), custom_call_target="tpu_custom_call" | custom-call | flops 1000000000 | bytes 4000000 | tf_op jit(solution)/shard_map/query_grad/pallas_call | solution.py:550
  69.0 0.1 collective-permute-done.20.refs_11_
  69.1 0.0 collective-permute-start.22
  69.1 1.4 %collective-permute-done.23.refs_15_ = bf16[8,64,512]{2,1,0:T(8,128)(2,1)S(1)} collective-permute-done((bf16[8,64,512]{2,1,0:T(8,128)(2,1)}, bf16[8,64,512]{2,1,0:T(8,128)(2,1)S(1)}, u32[]{:S(2)}, u32[]{:S(2)}) %collective-permute-start.23) | collective-permute-done | bytes 524320 | tf_op jit(solution)/shard_map/ppermute | solution.py:416
  70.5 0.0 collective-permute-start.25
  70.6 16.4 %all_to_all.5.stats_all_ref = f32[32,16,128]{2,1,0:T(8,128)} all-to-all(f32[32,16,128]{2,1,0:T(8,128)S(1)} %copy-done.17), channel_id=1, replica_groups=mesh['reader'=4,'blk'=8] {'reader','blk'}, dimensions={0} | all-to-all | bytes 524288 | tf_op jit(solution)/shard_map/all_to_all | solution.py:548
  87.0 0.0 collective-permute-done.21.refs_12_
  87.0 0.0 collective-permute-done.24.refs_16_
  87.0 0.0 collective-permute-done.22.refs_13_
  87.0 0.8 copy-done.23
  87.8 0.2 copy-done.24
  88.0 0.2 copy-done.25
  88.2 0.8 copy-done.26
  89.0 5.6 %key_grad.1 = bf16[128,512]{1,0:T(8,128)(2,1)} custom-call(s32[69]{0:T(128)} %copy-done.19, bf16[128,512]{1,0:T(8,128)(2,1)} %get-tuple-element.30.key_hbm, bf16[128,512]{1,0:T(8,128)(2,1)} %get-tuple-element.31.value_hbm, bf16[512,512]{1,0:T(8,128)(2,1)} %wq_hbm.3, bf16[512,512]{1,0:T(8,128)(2,1)} %get-tuple-element.32.wkt_hbm, ...), custom_call_target="tpu_custom_call" | custom-call | flops 1000000000 | bytes 4000000 | tf_op jit(solution)/shard_map/key_grad/pallas_call | solution.py:569
  (83 shorter events, 0.4 us)
Async XLA Ops:
  1.3 7.4 %copy-start.13 = (bf16[128,512]{1,0:T(8,128)(2,1)S(1)}, bf16[128,512]{1,0:T(8,128)(2,1)}, u32[]{:S(2)}) copy-start(bf16[128,512]{1,0:T(8,128)(2,1)} %cot_ref.1) | copy-start | bytes 393220
  2.9 9.0 %copy-start.20 = (bf16[1,144,512]{2,1,0:T(8,128)(2,1)S(1)}, bf16[1,144,512]{2,1,0:T(8,128)(2,1)}, u32[]{:S(2)}) copy-start(bf16[1,144,512]{2,1,0:T(8,128)(2,1)} %pack.1) | copy-start | bytes 442372
  2.9 13.2 %collective-permute-start.2 = (bf16[1,144,512]{2,1,0:T(8,128)(2,1)}, bf16[1,144,512]{2,1,0:T(8,128)(2,1)S(1)}, u32[]{:S(2)}, u32[]{:S(2)}) collective-permute-start(bf16[1,144,512]{2,1,0:T(8,128)(2,1)} %pack.1), channel_id=1, source_target_pairs={{0,6},{1,7},{2,4},{3,5},{4,2},{5,3},{6,0},{7,1},{8,14},{9,15},{10,... | collective-permute-start | bytes 442376 | tf_op jit(solution)/shard_map/ppermute | solution.py:416
  8.0 12.7 %collective-permute-start.1 = (bf16[1,144,512]{2,1,0:T(8,128)(2,1)}, bf16[1,144,512]{2,1,0:T(8,128)(2,1)S(1)}, u32[]{:S(2)}, u32[]{:S(2)}) collective-permute-start(bf16[1,144,512]{2,1,0:T(8,128)(2,1)} %pack.1), channel_id=1, source_target_pairs={{0,4},{1,5},{2,6},{3,7},{4,0},{5,1},{6,2},{7,3},{8,12},{9,13},{10,... | collective-permute-start | bytes 442376 | tf_op jit(solution)/shard_map/ppermute | solution.py:416
  8.0 12.7 %collective-permute-start = (bf16[1,144,512]{2,1,0:T(8,128)(2,1)}, bf16[1,144,512]{2,1,0:T(8,128)(2,1)S(1)}, u32[]{:S(2)}, u32[]{:S(2)}) collective-permute-start(bf16[1,144,512]{2,1,0:T(8,128)(2,1)} %pack.1), channel_id=1, source_target_pairs={{0,2},{1,3},{2,0},{3,1},{4,6},{5,7},{6,4},{7,5},{8,10},{9,11},{10,... | collective-permute-start | bytes 442376 | tf_op jit(solution)/shard_map/ppermute | solution.py:416
  8.7 4.3 %collective-permute-start.9 = (bf16[1,64,512]{2,1,0:T(8,128)(2,1)S(1)}, bf16[1,64,512]{2,1,0:T(8,128)(2,1)S(1)}, u32[]{:S(2)}, u32[]{:S(2)}) collective-permute-start(bf16[1,64,512]{2,1,0:T(8,128)(2,1)S(1)} %get-tuple-element.60), channel_id=1, source_target_pairs={{0,16},{1,17},{2,18},{3,19},{4,20},{5,21},{6,22},{7,23},{8,24},{9,... | collective-permute-start | bytes 196616 | tf_op jit(solution)/shard_map/ppermute | solution.py:416
  10.4 5.2 %collective-permute-start.8 = (bf16[1,64,512]{2,1,0:T(8,128)(2,1)S(1)}, bf16[1,64,512]{2,1,0:T(8,128)(2,1)S(1)}, u32[]{:S(2)}, u32[]{:S(2)}) collective-permute-start(bf16[1,64,512]{2,1,0:T(8,128)(2,1)S(1)} %get-tuple-element.61), channel_id=1, source_target_pairs={{0,8},{1,9},{2,10},{3,11},{4,12},{5,13},{6,14},{7,15},{8,0},{9,1},... | collective-permute-start | bytes 196616 | tf_op jit(solution)/shard_map/ppermute | solution.py:416
  13.0 8.7 %collective-permute-start.6 = (bf16[1,144,512]{2,1,0:T(8,128)(2,1)S(1)}, bf16[1,144,512]{2,1,0:T(8,128)(2,1)S(1)}, u32[]{:S(2)}, u32[]{:S(2)}) collective-permute-start(bf16[1,144,512]{2,1,0:T(8,128)(2,1)S(1)} %copy-done.20), channel_id=1, source_target_pairs={{0,24},{1,25},{2,26},{3,27},{4,28},{5,29},{6,30},{7,31},{8,16},{9,... | collective-permute-start | bytes 442376 | tf_op jit(solution)/shard_map/ppermute | solution.py:416
  15.6 6.1 %collective-permute-start.5 = (bf16[1,144,512]{2,1,0:T(8,128)(2,1)S(1)}, bf16[1,144,512]{2,1,0:T(8,128)(2,1)S(1)}, u32[]{:S(2)}, u32[]{:S(2)}) collective-permute-start(bf16[1,144,512]{2,1,0:T(8,128)(2,1)S(1)} %copy-done.20), channel_id=1, source_target_pairs={{0,16},{1,17},{2,18},{3,19},{4,20},{5,21},{6,22},{7,23},{8,24},{9,... | collective-permute-start | bytes 442376 | tf_op jit(solution)/shard_map/ppermute | solution.py:416
  16.1 0.7 copy-start.27
  16.1 5.6 %collective-permute-start.4 = (bf16[1,144,512]{2,1,0:T(8,128)(2,1)S(1)}, bf16[1,144,512]{2,1,0:T(8,128)(2,1)S(1)}, u32[]{:S(2)}, u32[]{:S(2)}) collective-permute-start(bf16[1,144,512]{2,1,0:T(8,128)(2,1)S(1)} %copy-done.20), channel_id=1, source_target_pairs={{0,8},{1,9},{2,10},{3,11},{4,12},{5,13},{6,14},{7,15},{8,0},{9,1},... | collective-permute-start | bytes 442376 | tf_op jit(solution)/shard_map/ppermute | solution.py:416
  20.7 0.9 slice-start
  21.6 3.7 %copy-start.28 = (bf16[1,144,512]{2,1,0:T(8,128)(2,1)S(1)}, bf16[1,144,512]{2,1,0:T(8,128)(2,1)}, u32[]{:S(2)}) copy-start(bf16[1,144,512]{2,1,0:T(8,128)(2,1)} %copy-done.27) | copy-start | bytes 442372
  21.7 36.2 %copy-start.1 = (bf16[3,128,512]{2,1,0:T(8,128)(2,1)}, bf16[3,128,512]{2,1,0:T(8,128)(2,1)S(1)}, u32[]{:S(2)}) copy-start(bf16[3,128,512]{2,1,0:T(8,128)(2,1)S(1)} %pad_maximum_fusion.3.refs_2_) | copy-start | bytes 1179652
  21.7 24.8 %collective-permute-start.12 = (bf16[3,128,512]{2,1,0:T(8,128)(2,1)S(1)}, bf16[3,128,512]{2,1,0:T(8,128)(2,1)S(1)}, u32[]{:S(2)}, u32[]{:S(2)}) collective-permute-start(bf16[3,128,512]{2,1,0:T(8,128)(2,1)S(1)} %pad_maximum_fusion.3.refs_2_), channel_id=1, source_target_pairs={{0,24},{1,25},{2,26},{3,27},{4,28},{5,29},{6,30},{7,31},{8,16},{9,... | collective-permute-start | bytes 1179656 | tf_op jit(solution)/shard_map/ppermute | solution.py:416
  24.2 22.9 %collective-permute-start.11 = (bf16[3,128,512]{2,1,0:T(8,128)(2,1)S(1)}, bf16[3,128,512]{2,1,0:T(8,128)(2,1)S(1)}, u32[]{:S(2)}, u32[]{:S(2)}) collective-permute-start(bf16[3,128,512]{2,1,0:T(8,128)(2,1)S(1)} %pad_maximum_fusion.3.refs_2_), channel_id=1, source_target_pairs={{0,16},{1,17},{2,18},{3,19},{4,20},{5,21},{6,22},{7,23},{8,24},{9,... | collective-permute-start | bytes 1179656 | tf_op jit(solution)/shard_map/ppermute | solution.py:416
  24.8 22.5 %collective-permute-start.10 = (bf16[3,128,512]{2,1,0:T(8,128)(2,1)S(1)}, bf16[3,128,512]{2,1,0:T(8,128)(2,1)S(1)}, u32[]{:S(2)}, u32[]{:S(2)}) collective-permute-start(bf16[3,128,512]{2,1,0:T(8,128)(2,1)S(1)} %pad_maximum_fusion.3.refs_2_), channel_id=1, source_target_pairs={{0,8},{1,9},{2,10},{3,11},{4,12},{5,13},{6,14},{7,15},{8,0},{9,1},... | collective-permute-start | bytes 1179656 | tf_op jit(solution)/shard_map/ppermute | solution.py:416
  25.3 1.6 %collective-permute-start.3 = (bf16[4,16,128]{2,1,0:T(8,128)(2,1)S(1)}, bf16[4,16,128]{2,1,0:T(8,128)(2,1)S(1)}, u32[]{:S(2)}, u32[]{:S(2)}) collective-permute-start(bf16[4,16,128]{2,1,0:T(8,128)(2,1)S(1)} %pad_maximum_fusion.5), channel_id=1, source_target_pairs={{0,1},{1,0},{2,3},{3,2},{4,5},{5,4},{6,7},{7,6},{8,9},{9,8},{10,11... | collective-permute-start | bytes 49160 | tf_op jit(solution)/shard_map/ppermute | solution.py:416
  25.6 32.3 %copy-start = (bf16[4,128,512]{2,1,0:T(8,128)(2,1)}, bf16[4,128,512]{2,1,0:T(8,128)(2,1)S(1)}, u32[]{:S(2)}) copy-start(bf16[4,128,512]{2,1,0:T(8,128)(2,1)S(1)} %pad_maximum_fusion.refs_0_) | copy-start | bytes 1572868
  26.9 0.6 copy-start.19
  27.5 19.0 %collective-permute-start.18 = (bf16[4,64,512]{2,1,0:T(8,128)(2,1)S(1)}, bf16[4,64,512]{2,1,0:T(8,128)(2,1)S(1)}, u32[]{:S(2)}, u32[]{:S(2)}) collective-permute-start(bf16[4,64,512]{2,1,0:T(8,128)(2,1)S(1)} %pad_maximum_fusion.4), channel_id=1, source_target_pairs={{0,2},{1,3},{2,0},{3,1},{4,6},{5,7},{6,4},{7,5},{8,10},{9,11},{10,... | collective-permute-start | bytes 786440 | tf_op jit(solution)/shard_map/ppermute | solution.py:416
  30.1 11.8 %collective-permute-start.17 = (bf16[4,64,512]{2,1,0:T(8,128)(2,1)S(1)}, bf16[4,64,512]{2,1,0:T(8,128)(2,1)S(1)}, u32[]{:S(2)}, u32[]{:S(2)}) collective-permute-start(bf16[4,64,512]{2,1,0:T(8,128)(2,1)S(1)} %pad_maximum_fusion.4), channel_id=1, source_target_pairs={{0,4},{1,5},{2,6},{3,7},{4,0},{5,1},{6,2},{7,3},{8,12},{9,13},{10,... | collective-permute-start | bytes 786440 | tf_op jit(solution)/shard_map/ppermute | solution.py:416
  33.9 24.0 %copy-start.18 = (s32[133]{0:T(256)}, s32[133]{0:T(256)S(1)}, u32[]{:S(2)}) copy-start(s32[133]{0:T(256)S(1)} %query_work.1.work_ref) | copy-start | bytes 1600
  41.9 10.7 %collective-permute-start.19 = (bf16[4,64,512]{2,1,0:T(8,128)(2,1)S(1)}, bf16[4,64,512]{2,1,0:T(8,128)(2,1)S(1)}, u32[]{:S(2)}, u32[]{:S(2)}) collective-permute-start(bf16[4,64,512]{2,1,0:T(8,128)(2,1)S(1)} %collective-permute-done.17), channel_id=1, source_target_pairs={{0,2},{1,3},{2,0},{3,1},{4,6},{5,7},{6,4},{7,5},{8,10},{9,11},{10,... | collective-permute-start | bytes 786440 | tf_op jit(solution)/shard_map/ppermute | solution.py:416
  46.5 9.8 %collective-permute-start.7 = (bf16[4,128,512]{2,1,0:T(8,128)(2,1)S(1)}, bf16[4,128,512]{2,1,0:T(8,128)(2,1)S(1)}, u32[]{:S(2)}, u32[]{:S(2)}) collective-permute-start(bf16[4,128,512]{2,1,0:T(8,128)(2,1)S(1)} %pad_maximum_fusion.refs_0_), channel_id=1, source_target_pairs={{0,1},{1,0},{2,3},{3,2},{4,5},{5,4},{6,7},{7,6},{8,9},{9,8},{10,11... | collective-permute-start | bytes 1572872 | tf_op jit(solution)/shard_map/ppermute | solution.py:416
  46.6 11.3 %copy-start.5 = (bf16[3,128,512]{2,1,0:T(8,128)(2,1)}, bf16[3,128,512]{2,1,0:T(8,128)(2,1)S(1)}, u32[]{:S(2)}) copy-start(bf16[3,128,512]{2,1,0:T(8,128)(2,1)S(1)} %collective-permute-done.12.refs_5_) | copy-start | bytes 1179652
  46.6 7.7 %collective-permute-start.13 = (bf16[3,128,512]{2,1,0:T(8,128)(2,1)S(1)}, bf16[3,128,512]{2,1,0:T(8,128)(2,1)S(1)}, u32[]{:S(2)}, u32[]{:S(2)}) collective-permute-start(bf16[3,128,512]{2,1,0:T(8,128)(2,1)S(1)} %pad_maximum_fusion.3.refs_2_), channel_id=1, source_target_pairs={{0,1},{1,0},{2,3},{3,2},{4,5},{5,4},{6,7},{7,6},{8,9},{9,8},{10,11... | collective-permute-start | bytes 1179656 | tf_op jit(solution)/shard_map/ppermute | solution.py:416
  47.2 10.8 %copy-start.6 = (bf16[3,128,512]{2,1,0:T(8,128)(2,1)}, bf16[3,128,512]{2,1,0:T(8,128)(2,1)S(1)}, u32[]{:S(2)}) copy-start(bf16[3,128,512]{2,1,0:T(8,128)(2,1)S(1)} %collective-permute-done.11.refs_4_) | copy-start | bytes 1179652
  47.2 10.7 %collective-permute-start.16 = (bf16[3,128,512]{2,1,0:T(8,128)(2,1)S(1)}, bf16[3,128,512]{2,1,0:T(8,128)(2,1)S(1)}, u32[]{:S(2)}, u32[]{:S(2)}) collective-permute-start(bf16[3,128,512]{2,1,0:T(8,128)(2,1)S(1)} %collective-permute-done.12.refs_5_), channel_id=1, source_target_pairs={{0,1},{1,0},{2,3},{3,2},{4,5},{5,4},{6,7},{7,6},{8,9},{9,8},{10,11... | collective-permute-start | bytes 1179656 | tf_op jit(solution)/shard_map/ppermute | solution.py:416
  47.3 10.7 %copy-start.7 = (bf16[3,128,512]{2,1,0:T(8,128)(2,1)}, bf16[3,128,512]{2,1,0:T(8,128)(2,1)S(1)}, u32[]{:S(2)}) copy-start(bf16[3,128,512]{2,1,0:T(8,128)(2,1)S(1)} %collective-permute-done.10.refs_3_) | copy-start | bytes 1179652
  47.3 10.6 %collective-permute-start.15 = (bf16[3,128,512]{2,1,0:T(8,128)(2,1)S(1)}, bf16[3,128,512]{2,1,0:T(8,128)(2,1)S(1)}, u32[]{:S(2)}, u32[]{:S(2)}) collective-permute-start(bf16[3,128,512]{2,1,0:T(8,128)(2,1)S(1)} %collective-permute-done.11.refs_4_), channel_id=1, source_target_pairs={{0,1},{1,0},{2,3},{3,2},{4,5},{5,4},{6,7},{7,6},{8,9},{9,8},{10,11... | collective-permute-start | bytes 1179656 | tf_op jit(solution)/shard_map/ppermute | solution.py:416
  52.6 5.3 %collective-permute-start.14 = (bf16[3,128,512]{2,1,0:T(8,128)(2,1)S(1)}, bf16[3,128,512]{2,1,0:T(8,128)(2,1)S(1)}, u32[]{:S(2)}, u32[]{:S(2)}) collective-permute-start(bf16[3,128,512]{2,1,0:T(8,128)(2,1)S(1)} %collective-permute-done.10.refs_3_), channel_id=1, source_target_pairs={{0,1},{1,0},{2,3},{3,2},{4,5},{5,4},{6,7},{7,6},{8,9},{9,8},{10,11... | collective-permute-start | bytes 1179656 | tf_op jit(solution)/shard_map/ppermute | solution.py:416
  52.6 5.4 %copy-start.12 = (bf16[512,512]{1,0:T(8,128)(2,1)S(1)}, bf16[512,512]{1,0:T(8,128)(2,1)}, u32[]{:S(2)}) copy-start(bf16[512,512]{1,0:T(8,128)(2,1)} %get-tuple-element.25.wvt_ref.wvt_hbm) | copy-start | bytes 1572868
  52.6 5.4 %copy-start.14 = (bf16[128,512]{1,0:T(8,128)(2,1)S(1)}, bf16[128,512]{1,0:T(8,128)(2,1)}, u32[]{:S(2)}) copy-start(bf16[128,512]{1,0:T(8,128)(2,1)} %cot_ref.1) | copy-start | bytes 393220
  52.6 5.3 %copy-start.15 = (bf16[4,128,256]{2,1,0:T(8,128)(2,1)S(1)}, bf16[4,128,256]{2,1,0:T(8,128)(2,1)}, u32[]{:S(2)}) copy-start(bf16[4,128,256]{2,1,0:T(8,128)(2,1)} %get-tuple-element.24.stack_ref.stack_hbm) | copy-start | bytes 786436
  53.5 4.5 %copy-start.2 = (bf16[512,512]{1,0:T(8,128)(2,1)S(1)}, bf16[512,512]{1,0:T(8,128)(2,1)}, u32[]{:S(2)}) copy-start(bf16[512,512]{1,0:T(8,128)(2,1)} %wk_hbm.3) | copy-start | bytes 1572868
  53.5 4.5 %copy-start.4 = (s32[240,128,4]{1,2,0:T(4,128)S(1)}, s32[240,128,4]{1,2,0:T(4,128)}, u32[]{:S(2)}) copy-start(s32[240,128,4]{1,2,0:T(4,128)} %param.15) | copy-start | bytes 1474564
  54.3 7.9 %copy-start.8 = (bf16[3,128,512]{2,1,0:T(8,128)(2,1)}, bf16[3,128,512]{2,1,0:T(8,128)(2,1)S(1)}, u32[]{:S(2)}) copy-start(bf16[3,128,512]{2,1,0:T(8,128)(2,1)S(1)} %collective-permute-done.13.refs_6_) | copy-start | bytes 1179652
  54.3 14.7 %collective-permute-start.20 = (bf16[8,64,512]{2,1,0:T(8,128)(2,1)}, bf16[8,64,512]{2,1,0:T(8,128)(2,1)S(1)}, u32[]{:S(2)}, u32[]{:S(2)}) collective-permute-start(bf16[8,64,512]{2,1,0:T(8,128)(2,1)} %pad_maximum_fusion.1.refs_10_), channel_id=1, source_target_pairs={{0,16},{1,17},{2,18},{3,19},{4,20},{5,21},{6,22},{7,23},{8,24},{9,... | collective-permute-start | bytes 1572872 | tf_op jit(solution)/shard_map/ppermute | solution.py:416
  56.3 6.0 %copy-start.3 = (bf16[4,128,512]{2,1,0:T(8,128)(2,1)}, bf16[4,128,512]{2,1,0:T(8,128)(2,1)S(1)}, u32[]{:S(2)}) copy-start(bf16[4,128,512]{2,1,0:T(8,128)(2,1)S(1)} %collective-permute-done.7.refs_1_) | copy-start | bytes 1572868
  56.3 14.3 %collective-permute-start.23 = (bf16[8,64,512]{2,1,0:T(8,128)(2,1)}, bf16[8,64,512]{2,1,0:T(8,128)(2,1)S(1)}, u32[]{:S(2)}, u32[]{:S(2)}) collective-permute-start(bf16[8,64,512]{2,1,0:T(8,128)(2,1)} %pad_maximum_fusion.2.refs_14_), channel_id=1, source_target_pairs={{0,8},{1,9},{2,10},{3,11},{4,12},{5,13},{6,14},{7,15},{8,0},{9,1},... | collective-permute-start | bytes 1572872 | tf_op jit(solution)/shard_map/ppermute | solution.py:416
  57.8 4.4 %copy-start.9 = (bf16[3,128,512]{2,1,0:T(8,128)(2,1)}, bf16[3,128,512]{2,1,0:T(8,128)(2,1)S(1)}, u32[]{:S(2)}) copy-start(bf16[3,128,512]{2,1,0:T(8,128)(2,1)S(1)} %collective-permute-done.16.refs_9_) | copy-start | bytes 1179652
  57.8 4.4 %copy-start.10 = (bf16[3,128,512]{2,1,0:T(8,128)(2,1)}, bf16[3,128,512]{2,1,0:T(8,128)(2,1)S(1)}, u32[]{:S(2)}) copy-start(bf16[3,128,512]{2,1,0:T(8,128)(2,1)S(1)} %collective-permute-done.15.refs_8_) | copy-start | bytes 1179652
  57.9 4.4 %copy-start.11 = (bf16[3,128,512]{2,1,0:T(8,128)(2,1)}, bf16[3,128,512]{2,1,0:T(8,128)(2,1)S(1)}, u32[]{:S(2)}) copy-start(bf16[3,128,512]{2,1,0:T(8,128)(2,1)S(1)} %collective-permute-done.14.refs_7_) | copy-start | bytes 1179652
  62.3 0.7 copy-start.16
  63.0 7.6 %copy-start.17 = (f32[32,16,128]{2,1,0:T(8,128)S(1)}, f32[32,16,128]{2,1,0:T(8,128)}, u32[]{:S(2)}) copy-start(f32[32,16,128]{2,1,0:T(8,128)} %copy-done.16) | copy-start | bytes 786436
  63.0 24.0 %collective-permute-start.21 = (bf16[8,64,512]{2,1,0:T(8,128)(2,1)}, bf16[8,64,512]{2,1,0:T(8,128)(2,1)S(1)}, u32[]{:S(2)}, u32[]{:S(2)}) collective-permute-start(bf16[8,64,512]{2,1,0:T(8,128)(2,1)} %pad_maximum_fusion.1.refs_10_), channel_id=1, source_target_pairs={{0,1},{1,0},{2,3},{3,2},{4,5},{5,4},{6,7},{7,6},{8,9},{9,8},{10,11... | collective-permute-start | bytes 1572872 | tf_op jit(solution)/shard_map/ppermute | solution.py:416
  63.0 24.0 %collective-permute-start.24 = (bf16[8,64,512]{2,1,0:T(8,128)(2,1)}, bf16[8,64,512]{2,1,0:T(8,128)(2,1)S(1)}, u32[]{:S(2)}, u32[]{:S(2)}) collective-permute-start(bf16[8,64,512]{2,1,0:T(8,128)(2,1)} %pad_maximum_fusion.2.refs_14_), channel_id=1, source_target_pairs={{0,1},{1,0},{2,3},{3,2},{4,5},{5,4},{6,7},{7,6},{8,9},{9,8},{10,11... | collective-permute-start | bytes 1572872 | tf_op jit(solution)/shard_map/ppermute | solution.py:416
  69.1 17.9 %copy-start.21 = (bf16[8,64,512]{2,1,0:T(8,128)(2,1)}, bf16[8,64,512]{2,1,0:T(8,128)(2,1)S(1)}, u32[]{:S(2)}) copy-start(bf16[8,64,512]{2,1,0:T(8,128)(2,1)S(1)} %collective-permute-done.20.refs_11_) | copy-start | bytes 1572868
  69.1 17.9 %collective-permute-start.22 = (bf16[8,64,512]{2,1,0:T(8,128)(2,1)S(1)}, bf16[8,64,512]{2,1,0:T(8,128)(2,1)S(1)}, u32[]{:S(2)}, u32[]{:S(2)}) collective-permute-start(bf16[8,64,512]{2,1,0:T(8,128)(2,1)S(1)} %collective-permute-done.20.refs_11_), channel_id=1, source_target_pairs={{0,1},{1,0},{2,3},{3,2},{4,5},{5,4},{6,7},{7,6},{8,9},{9,8},{10,11... | collective-permute-start | bytes 1572872 | tf_op jit(solution)/shard_map/ppermute | solution.py:416
  70.5 16.5 %copy-start.22 = (bf16[8,64,512]{2,1,0:T(8,128)(2,1)}, bf16[8,64,512]{2,1,0:T(8,128)(2,1)S(1)}, u32[]{:S(2)}) copy-start(bf16[8,64,512]{2,1,0:T(8,128)(2,1)S(1)} %collective-permute-done.23.refs_15_) | copy-start | bytes 1572868
  70.5 16.5 %collective-permute-start.25 = (bf16[8,64,512]{2,1,0:T(8,128)(2,1)S(1)}, bf16[8,64,512]{2,1,0:T(8,128)(2,1)S(1)}, u32[]{:S(2)}, u32[]{:S(2)}) collective-permute-start(bf16[8,64,512]{2,1,0:T(8,128)(2,1)S(1)} %collective-permute-done.23.refs_15_), channel_id=1, source_target_pairs={{0,1},{1,0},{2,3},{3,2},{4,5},{5,4},{6,7},{7,6},{8,9},{9,8},{10,11... | collective-permute-start | bytes 1572872 | tf_op jit(solution)/shard_map/ppermute | solution.py:416
  87.0 0.8 copy-start.23
  87.0 1.0 %copy-start.24 = (bf16[8,64,512]{2,1,0:T(8,128)(2,1)}, bf16[8,64,512]{2,1,0:T(8,128)(2,1)S(1)}, u32[]{:S(2)}) copy-start(bf16[8,64,512]{2,1,0:T(8,128)(2,1)S(1)} %collective-permute-done.24.refs_16_) | copy-start | bytes 1572868
  87.0 1.2 %copy-start.25 = (bf16[8,64,512]{2,1,0:T(8,128)(2,1)}, bf16[8,64,512]{2,1,0:T(8,128)(2,1)S(1)}, u32[]{:S(2)}) copy-start(bf16[8,64,512]{2,1,0:T(8,128)(2,1)S(1)} %collective-permute-done.22.refs_13_) | copy-start | bytes 1572868
  88.2 0.8 copy-start.26
